TPU v7x, 512 devices: a whole 4x8x8 slice. The times are simulated.
512 devices in a mesh: tp: 8 (over x, y_hi), dp: 16 (over z, core), edp: 4 (over y_lo).
Axes of the slice: x: 4, y: 8 (y_hi: 2, y_lo: 4; y = y_hi * 4 + y_lo), z: 8, core: 2. Of those that a mesh axis runs over, the one named last changes fastest.
Arguments:
- grad_out: bfloat16 [8192, 4096], P(('dp', 'edp')), may hold values from -0.29882812 to 0.29882812
- routes: int32 [8192, 8], P(('dp', 'edp')), may hold values from 0 to 63, all different within a row; in each aligned block of 128 rows (0 to 127, 128 to 255, ...) at most 20 rows name the same one
- gates: bfloat16 [8192, 8], P(('dp', 'edp')), may hold values from 0.099609375 to 1
- hidden: bfloat16 [64, 1536, 1280], P(('dp', 'edp'), 'tp'), may hold values from -40 to 40
- w_down: bfloat16 [64, 1536, 4096], P(('dp', 'edp'), 'tp'), may hold values from -0.15625 to 0.15625
Outputs:
- down_grad: bfloat16 [64, 1536, 4096], P(('dp', 'edp'), 'tp')
- gate_grad: float32 [8192, 8], P(('dp', 'edp'))
Inputs may be any that keep to these rules, and one draw needn't show every extreme that they name: `routes`: each row names 8 different experts. Within the 128 rows of one index of dp+edp no expert is named more than 20 times, and in every draw some expert is named exactly 20 times in some block.
All inputs are finite; a program needn't handle non-finite values.
Results may differ from a plain program's by a relative error of at most 0.0049.
Values may be sent and summed in bfloat16 or wider, within the bound.
A program may use at most 128 MiB of HBM per device.

v0:
```python
import math

import jax
import jax.numpy as jnp
from jax import lax
from jax.sharding import PartitionSpec as P

clip_ratio = 0.25


def slot_plan(routes, sources, capacity):
    flat_routes = routes.reshape(-1)
    pair_count = flat_routes.shape[0]
    onehot = (flat_routes[:, None] == jnp.arange(sources, dtype=jnp.int32)[None, :]).astype(
        jnp.int32
    )
    before = jnp.cumsum(onehot, axis=0) - onehot
    position = jnp.sum(before * onehot, axis=1)
    target = flat_routes * capacity + position
    filler = (
        jnp.zeros((sources * capacity,), jnp.int32)
        .at[target]
        .set(jnp.arange(pair_count, dtype=jnp.int32))
    )
    filled = jnp.zeros((sources * capacity,), jnp.int32).at[target].set(1)
    return (target, filler, filled)


def dense_products(row_block, gate_rows, hidden_part, weight_part):
    back_proj = lax.dot_general(
        weight_part, row_block, (((1,), (1,)), ((), ())), preferred_element_type=jnp.float32
    )
    partial_value = jnp.sum(hidden_part.astype(jnp.float32) * back_proj, axis=0)
    scaled = (hidden_part.astype(jnp.float32) * gate_rows.astype(jnp.float32)[None, :]).astype(
        jnp.bfloat16
    )
    weight_grad = jnp.dot(scaled, row_block, preferred_element_type=jnp.float32)
    return (weight_grad, partial_value)


def per_device(grad_out, routes, gates, hidden, w_down):
    sources = lax.axis_size("dp") * lax.axis_size("edp")
    slot_total = hidden.shape[2]
    capacity = slot_total // sources
    model_width = grad_out.shape[1]
    target, filler, filled = slot_plan(routes, sources, capacity)
    slot_live = filled.astype(jnp.bfloat16)
    tokens_of = filler // routes.shape[1]
    gate_slots = (gates.reshape(-1)[filler] * slot_live).reshape(sources, capacity)
    outgoing = (grad_out[tokens_of] * slot_live[:, None]).reshape(sources, capacity, model_width)
    arrived, gate_in = (
        lax.all_to_all(outgoing, ("dp", "edp"), split_axis=0, concat_axis=0, tiled=True),
        lax.all_to_all(gate_slots, ("dp", "edp"), split_axis=0, concat_axis=0, tiled=True),
    )
    row_block = arrived.reshape(slot_total, model_width)
    gate_rows = gate_in.reshape(slot_total)
    hidden_part = hidden[0]
    weight_part = w_down[0]
    weight_grad, partial_value = dense_products(row_block, gate_rows, hidden_part, weight_part)
    returned = lax.all_to_all(
        partial_value.reshape(sources, capacity),
        ("dp", "edp"),
        split_axis=0,
        concat_axis=0,
        tiled=True,
    )
    picked = returned.reshape(-1)[target].reshape(routes.shape)
    gate_grad = lax.psum(picked, "tp")
    squares = jnp.sum(weight_grad * weight_grad)
    total_squares = lax.psum(squares, ("tp", "dp", "edp"))
    entries = weight_grad.shape[0] * weight_grad.shape[1] * lax.axis_size("tp") * sources
    clip_limit = clip_ratio * math.sqrt(entries)
    factor = jnp.minimum(1.0, clip_limit / (jnp.sqrt(total_squares) + 1e-06))
    down_grad = (weight_grad * factor).astype(jnp.bfloat16)[None]
    return (down_grad, gate_grad)


def solution(mesh):
    in_specs = (
        P(("dp", "edp"), None),
        P(("dp", "edp"), None),
        P(("dp", "edp"), None),
        P(("dp", "edp"), "tp", None),
        P(("dp", "edp"), "tp", None),
    )
    out_specs = (P(("dp", "edp"), "tp", None), P(("dp", "edp"), None))
    return jax.shard_map(
        per_device, mesh=mesh, in_specs=in_specs, out_specs=out_specs, check_vma=False
    )
```

profile of v0, /device:TPU:1, one launch (start us, length us, event | category | flops | bytes accessed | tf_op | source)
XLA Modules:
  0.0 705.4 jit_solution(1040019025118233693)
XLA Ops:
  0.7 0.9 copy.16
  2.5 18.0 %reduce-window.6 = s32[64,8,128]{2,1,0:T(8,128)S(1)} reduce-window(s32[64,8,128]{2,1,0:T(8,128)S(1)} %fusion.14, s32[]{:T(128)} %constant.13.clone.1), window={size=1x1x128 pad=0_0x0_0x127_0}, to_apply=%region_0.0 | reduce-window | flops 8323072 | bytes 524292 | tf_op jit(solution)/shard_map/reduce-window
  21.4 4.3 scatter_custom_fusion
  25.7 0.8 copy.14
  26.6 4.3 scatter_custom_fusion.1
  31.0 8.0 %gather_fusion = bf16[1280]{0:T(1024)(128)(2,1)S(1)} fusion(bf16[1024]{0:T(1024)(128)(2,1)S(1)} %reshape.97, s32[2048]{0:T(1024)S(1)} %get-tuple-element.13), kind=kCustom, calls=%fused_computation | custom fusion | bytes 10240 | tf_op jit(solution)/shard_map/gather | solution.py:49
  38.9 0.7 all_to_all.20
  39.7 15.4 %all-to-all-start = ((bf16[64,1,20]{2,1,0:T(2,128)(2,1)}), bf16[64,1,20]{2,1,0:T(2,128)(2,1)S(1)}, u32[]{:S(2)}, u32[]{:S(2)}) async-start(bf16[64,1,20]{2,1,0:T(2,128)(2,1)} %all_to_all.20), calls=%async_computation | async-start | bytes 65536 | tf_op jit(solution)/shard_map/all_to_all | solution.py:53
  55.2 8.4 %gather_fusion.1 = bf16[1280,4096]{1,0:T(8,128)(2,1)} fusion(bf16[128,4096]{1,0:T(8,128)(2,1)S(1)} %copy-done.1, s32[2048]{0:T(1024)S(1)} %get-tuple-element.12), kind=kCustom, calls=%fused_computation.1 | custom fusion | bytes 20976640 | tf_op jit(solution)/shard_map/gather | solution.py:50
  63.6 13.8 %gather.13 = bf16[64,20,4096]{2,1,0:T(8,128)(2,1)} reshape(bf16[1280,4096]{1,0:T(8,128)(2,1)} %gather_fusion.1) | data formatting | bytes 20971520 | tf_op jit(solution)/shard_map/gather | solution.py:50
  77.4 10.7 %broadcast_multiply_fusion = bf16[64,20,4096]{2,1,0:T(8,128)(2,1)} fusion(bf16[64,20,4096]{2,1,0:T(8,128)(2,1)} %gather.13, bf16[64,20]{1,0:T(8,128)(2,1)S(1)} %mul.61), kind=kLoop, calls=%fused_computation.5 | loop fusion | flops 5242880 | bytes 20974080 | tf_op jit(solution)/shard_map/mul | solution.py:50
  88.1 10.7 %all-to-all-start.1 = ((bf16[64,20,4096]{2,1,0:T(8,128)(2,1)}), bf16[64,20,4096]{2,1,0:T(8,128)(2,1)}, u32[]{:S(2)}, u32[]{:S(2)}) async-start(bf16[64,20,4096]{2,1,0:T(8,128)(2,1)} %broadcast_multiply_fusion), calls=%async_computation.1 | async-start | bytes 25165824 | tf_op jit(solution)/shard_map/all_to_all | solution.py:52
  99.1 327.1 %all-to-all-done.1 = bf16[64,20,4096]{2,1,0:T(8,128)(2,1)} async-done(((bf16[64,20,4096]{2,1,0:T(8,128)(2,1)}), bf16[64,20,4096]{2,1,0:T(8,128)(2,1)}, u32[]{:S(2)}, u32[]{:S(2)}) %all-to-all-start.1) | async-done | bytes 10485792 | tf_op jit(solution)/shard_map/all_to_all | solution.py:52
  426.2 14.0 %reshape.99 = bf16[1280,4096]{1,0:T(8,128)(2,1)} reshape(bf16[64,20,4096]{2,1,0:T(8,128)(2,1)} %all-to-all-done.1) | data formatting | bytes 20971520 | tf_op jit(solution)/shard_map/reshape | solution.py:55
  440.2 8.5 %multiply_reduce_fusion = (f32[]{:T(128)}, f32[192,4096]{1,0:T(8,128)}) fusion(bf16[1280,4096]{1,0:T(8,128)(2,1)} %reshape.99, bf16[1,192,1280]{2,1,0:T(8,128)(2,1)S(1)} %copy-done.2, f32[1280]{0:T(1024)S(1)} %reshape.102), kind=kOutput, calls=%fused_computation.7 | convolution fusion | flops 2015576064 | bytes 14128132 | tf_op jit(solution)/shard_map/dot_general | solution.py:37
  448.7 179.3 %psum.14 = f32[]{:T(128)} all-reduce(f32[]{:T(128)} %get-tuple-element.10), channel_id=1, replica_groups=mesh['tp'=8,'dp'=16,'edp'=4] {'tp','dp','edp'}, use_global_device_ids=true, to_apply=%region_6.7 | all-reduce | flops 1 | bytes 8 | tf_op jit(solution)/shard_map/psum | solution.py:70
  628.7 7.6 %fusion.3 = f32[1280]{0:T(1024)S(1)} fusion(bf16[1280,4096]{1,0:T(8,128)(2,1)} %reshape.99, bf16[1,192,4096]{2,1,0:T(8,128)(2,1)S(1)} %copy-done, bf16[1,192,1280]{2,1,0:T(8,128)(2,1)S(1)} %copy-done.2), kind=kOutput, calls=%fused_computation.12 | convolution fusion | flops 2014001920 | bytes 12555264 | tf_op jit(solution)/shard_map/dot_general | solution.py:30
  636.3 0.7 all_to_all.18
  637.0 7.3 %all-to-all-start.2 = ((f32[64,1,20]{2,1,0:T(1,128)}), f32[64,1,20]{2,1,0:T(1,128)S(1)}, u32[]{:S(2)}, u32[]{:S(2)}) async-start(f32[64,1,20]{2,1,0:T(1,128)} %bitcast.9), calls=%async_computation.2 | async-start | bytes 65536 | tf_op jit(solution)/shard_map/all_to_all | solution.py:60
  644.3 3.3 fusion.1
  647.6 6.1 all-to-all-done.2
  654.2 0.7 reduce.7
  655.1 6.2 gather_fusion.2
  661.3 43.4 %psum.15 = f32[128,8]{1,0:T(8,128)S(1)} all-reduce(f32[128,8]{1,0:T(8,128)S(1)} %reshape.101), channel_id=1, replica_groups=mesh['tp'=8,'dp'=16,'edp'=4] {'tp'}, use_global_device_ids=true, to_apply=%region_8.9 | all-reduce | flops 1024 | bytes 8192 | tf_op jit(solution)/shard_map/psum | solution.py:68
  (35 shorter events, 3.5 us)
Async XLA Ops:
  0.6 628.1 %copy-start = (bf16[1,192,4096]{2,1,0:T(8,128)(2,1)S(1)}, bf16[1,192,4096]{2,1,0:T(8,128)(2,1)}, u32[]{:S(2)}) copy-start(bf16[1,192,4096]{2,1,0:T(8,128)(2,1)} %param.9) | copy-start | bytes 4718596
  0.6 54.6 %copy-start.1 = (bf16[128,4096]{1,0:T(8,128)(2,1)S(1)}, bf16[128,4096]{1,0:T(8,128)(2,1)}, u32[]{:S(2)}) copy-start(bf16[128,4096]{1,0:T(8,128)(2,1)} %param.5) | copy-start | bytes 3145732
  39.7 48.4 %all-to-all-start = ((bf16[64,1,20]{2,1,0:T(2,128)(2,1)}), bf16[64,1,20]{2,1,0:T(2,128)(2,1)S(1)}, u32[]{:S(2)}, u32[]{:S(2)}) async-start(bf16[64,1,20]{2,1,0:T(2,128)(2,1)} %all_to_all.20), calls=%async_computation | async-start | bytes 65536 | tf_op jit(solution)/shard_map/all_to_all | solution.py:53
  88.1 338.1 %all-to-all-start.1 = ((bf16[64,20,4096]{2,1,0:T(8,128)(2,1)}), bf16[64,20,4096]{2,1,0:T(8,128)(2,1)}, u32[]{:S(2)}, u32[]{:S(2)}) async-start(bf16[64,20,4096]{2,1,0:T(8,128)(2,1)} %broadcast_multiply_fusion), calls=%async_computation.1 | async-start | bytes 25165824 | tf_op jit(solution)/shard_map/all_to_all | solution.py:52
  99.1 341.1 %copy-start.2 = (bf16[1,192,1280]{2,1,0:T(8,128)(2,1)S(1)}, bf16[1,192,1280]{2,1,0:T(8,128)(2,1)}, u32[]{:S(2)}) copy-start(bf16[1,192,1280]{2,1,0:T(8,128)(2,1)} %param.8) | copy-start | bytes 1474564
  637.0 16.7 %all-to-all-start.2 = ((f32[64,1,20]{2,1,0:T(1,128)}), f32[64,1,20]{2,1,0:T(1,128)S(1)}, u32[]{:S(2)}, u32[]{:S(2)}) async-start(f32[64,1,20]{2,1,0:T(1,128)} %bitcast.9), calls=%async_computation.2 | async-start | bytes 65536 | tf_op jit(solution)/shard_map/all_to_all | solution.py:60
where the time goes:
time: 712 us; the launch traced here: 705 us
  waiting for transfers between devices  333 us (47%)
  blocking collectives  223 us (31%)
  local copies, waits for them, and re-layouts  64.6 us (9%)
  other arithmetic  33.8 us (5%)
  starting transfers between devices  33.4 us (5%)
  matrix products  16 us (2%)
    all_to_all x1, waiting for transfers between devices, per_device(): lax.all_to_all(outgoing, ('dp', 'edp'), split_axis=0, concat_axis=0, tile...  327 us
    psum x1, blocking collectives, per_device(): total_squares = lax.psum(squares, ('tp', 'dp', 'edp'))  179 us
    psum x1, blocking collectives, per_device(): gate_grad = lax.psum(picked, 'tp')  43.4 us
    gather x2, local copies, waits for them, and re-layouts, per_device(): grad_out[tokens_of] * slot_live[:, None]  22.2 us
    another operation x3, other arithmetic  18.2 us
    all_to_all x1, starting transfers between devices, per_device(): lax.all_to_all(gate_slots, ('dp', 'edp'), split_axis=0, concat_axis=0, ti...  15.4 us
  transfers between devices with their start and end apart: 3, of which 2 were waited for; matrix products, arithmetic and copies ran while one was open for 5% of the time, Pallas kernels for 0%

commit v1 on v0

v1 whole, which is shorter than its diff:
```python
import functools
import math

import jax
import jax.numpy as jnp
from jax import lax
from jax.experimental import pallas as pl
from jax.experimental.pallas import tpu as pltpu
from jax.sharding import PartitionSpec as P

clip_ratio = 0.25

XS, HS, ZS, CS, YS = 4, 2, 8, 2, 4
NQ = 4
CAP = 20
MESH = pl.DeviceIdType.MESH
F32, BF16 = jnp.float32, jnp.bfloat16

K_Q, K_G, K_GY, K_PA, K_PB, K_PC, K_RY, K_RZ, K_GG = range(9)


def iota(shape, dim):
    return lax.broadcasted_iota(jnp.int32, shape, dim)


def kernel(
    routes_ref, gates_ref, grad_hbm, hid_hbm, w_hbm,
    out_hbm, total_ref, gg_ref,
    tok, sel, sendb, rows, qsend, qrecv, gsend, grecv, gsy, gtab,
    hraw, perm, hx, hs, hxt, wv, wgs, acc, pa, pb, pc, rsend, ry, rzs, rz, gg,
    loc, zs, zr, ys, yr, ws, wr, hsn, hr, osn, orc, sms, smr,
):
    E8 = CS * YS
    TPS = XS * HS
    EXP = ZS * E8
    TOK, TOP = routes_ref.shape[1], routes_ref.shape[0]
    FFD = hid_hbm.shape[1]
    SLOTS = hid_hbm.shape[2]
    DX = w_hbm.shape[2] // XS
    DQ = DX // NQ
    BLK = ZS * CAP
    GZ = min(4, ZS)
    HALF = ZS // 2

    tp = lax.axis_index("tp")
    dp = lax.axis_index("dp")
    y = lax.axis_index("edp")
    x, h = lax.div(tp, HS), lax.rem(tp, HS)
    z, c = lax.div(dp, CS), lax.rem(dp, CS)
    yy = h * YS + y
    me8 = c * YS + y

    def at_y(delta, core):
        there = lax.rem(yy + delta + HS * YS, HS * YS)
        ylo = lax.rem(there, YS)
        return (x * HS + lax.div(there, YS), z * CS + core, ylo), core * YS + ylo

    def at_z(delta):
        zz = lax.rem(z + delta + ZS, ZS)
        return (tp, zz * CS + c, y), zz

    def at_x(delta):
        xx = lax.rem(x + delta, XS)
        return (xx * HS + h, dp, y), xx

    def at_tp(delta):
        tt = lax.rem(tp + delta, TPS)
        return (tt, dp, y), tt

    far = 2 - 4 * c
    out_y = [at_y(0, 1 - c), at_y(1, 0), at_y(-1, 0), at_y(1, 1), at_y(-1, 1), at_y(2, 0), at_y(-2, 1)]
    back_y = out_y[:5] + [at_y(-far, 0), at_y(-far, 1)]
    peers_z = [at_z(i) for i in range(1, ZS)]
    peers_x = [at_x(i) for i in range(1, XS)]
    peers_tp = [at_tp(i) for i in range(1, TPS)]

    barrier = pltpu.get_barrier_semaphore()
    hello = [d for d, _ in peers_z] + [d for d, _ in peers_tp] + [d for d, _ in out_y]
    hello = hello + [at_y(-far, c)[0]]
    for d in hello:
        pl.semaphore_signal(barrier, inc=1, device_id=d, device_id_type=MESH)

    def col(start):
        return pl.ds(pl.multiple_of(start, DQ), DQ)

    def blk(start, size):
        return pl.ds(pl.multiple_of(start * size, size), size)

    get_h = pltpu.make_async_copy(hid_hbm.at[0], hraw, loc.at[0])
    get_h.start()
    get_t = [
        pltpu.make_async_copy(grad_hbm.at[:, col(x * DX + q * DQ)], tok.at[q, blk(z, TOK)], loc.at[1 + q])
        for q in range(NQ)
    ]
    for d in get_t:
        d.start()

    def own_w(q):
        return pltpu.make_async_copy(
            w_hbm.at[0, :, col(x * DX + q * DQ)], wv.at[q, blk(x, FFD)], loc.at[1 + NQ + q])

    for q in range(NQ):
        own_w(q).start()

    eidx = iota((EXP, TOK), 0)
    chosen = jnp.zeros((EXP, TOK), F32)
    gate_t = jnp.zeros((EXP, TOK), F32)
    gates_f = gates_ref[...].astype(F32)
    for k in range(TOP):
        hit = routes_ref[k:k + 1, :] == eidx
        chosen = jnp.where(hit, 1.0, chosen)
        gate_t = jnp.where(hit, gates_f[k:k + 1, :], gate_t)
    earlier = (iota((TOK, TOK), 0) < iota((TOK, TOK), 1)).astype(F32).astype(BF16)
    count = jnp.dot(chosen.astype(BF16), earlier, preferred_element_type=F32)
    qt = jnp.where(chosen > 0.5, count, -1.0)
    for i in range(ZS):
        qsend[i] = qt[i * E8:(i + 1) * E8]
    qrecv[z] = qsend[z]

    pl.semaphore_wait(barrier, len(hello))

    def small(kind, i, src, dst, mine, dev):
        return pltpu.make_async_remote_copy(
            src_ref=src, dst_ref=dst.at[mine], send_sem=sms.at[kind, i], recv_sem=smr.at[kind, mine],
            device_id=dev, device_id_type=MESH)

    def small_start(kind, peers, src_of, dst, mine):
        for i, (dev, there) in enumerate(peers):
            small(kind, i, src_of(there), dst, mine, dev).start()

    def small_wait(kind, peers, dst):
        for i, (dev, there) in enumerate(peers):
            small(kind, i, dst.at[there], dst, there, dev).wait_recv()

    def small_done(kind, peers, src_of, dst, mine):
        for i, (dev, there) in enumerate(peers):
            small(kind, i, src_of(there), dst, mine, dev).wait_send()

    def ring(q, block, right, i):
        dev = peers_z[0][0] if right else peers_z[ZS - 2][0]
        part = tok.at[q, blk(block, TOK)]
        return pltpu.make_async_remote_copy(
            src_ref=part, dst_ref=part, send_sem=zs.at[q, i], recv_sem=zr.at[q, block],
            device_id=dev, device_id_type=MESH)

    def zb(delta):
        return lax.rem(z + delta + ZS, ZS)

    sent = []

    def ring_step(q, s):
        ways = [True, False] if s < HALF else [q % 2 == 0]
        for right in ways:
            block = zb(-(s - 1)) if right else zb(s - 1)
            if s > 1:
                ring(q, block, right, 0).wait_recv()
            i = 2 * (s - 1) + (0 if right else 1)
            if s == HALF:
                i = 2 * (s - 1)
            d = ring(q, block, right, i)
            d.start()
            sent.append(d)

    def ring_end(q):
        if HALF > 1:
            left_over = zb(HALF - 1) if q % 2 == 0 else zb(-(HALF - 1))
            ring(q, left_over, True, 0).wait_recv()
        ring(q, zb(HALF), True, 0).wait_recv()

    def send_w(q, i):
        dev, there = peers_x[i]
        return pltpu.make_async_remote_copy(
            src_ref=w_hbm.at[0, :, col(there * DX + q * DQ)], dst_ref=wv.at[q, blk(x, FFD)],
            send_sem=ws.at[q, i], recv_sem=wr.at[q, x], device_id=dev, device_id_type=MESH)

    def send_h(i):
        dev, there = peers_x[i]
        part = hx.at[blk(x, FFD)]
        return pltpu.make_async_remote_copy(
            src_ref=part, dst_ref=part, send_sem=hsn.at[i], recv_sem=hr.at[x], device_id=dev, device_id_type=MESH)

    for q in range(NQ):
        if q < 1:
            get_t[q].wait()
            ring_step(q, 1)
    small_start(K_Q, peers_z, lambda there: qsend.at[there], qrecv, z)
    for i in range(XS - 1):
        send_w(0, i).start()

    lane = (iota((1, SLOTS), 1).astype(F32) + 0.5)
    group = jnp.floor(lane * (1.0 / BLK))
    inner = lane - group * BLK
    zpart = jnp.floor(inner * (1.0 / CAP))
    place = inner - zpart * CAP - 0.5
    native = (zpart * (E8 * CAP) + group * CAP + place).astype(jnp.int32)
    source = (group * ZS + zpart).astype(jnp.int32)
    place = place.astype(jnp.int32)

    PB = 128

    def build_perm(i, carry):
        perm[pl.ds(pl.multiple_of(i * PB, PB), PB), :] = (
            (iota((PB, SLOTS), 0) + i * PB) == native).astype(F32).astype(BF16)
        return carry

    lax.fori_loop(0, SLOTS // PB, build_perm, 0)
    get_h.wait()
    hx[blk(x, FFD), :] = jnp.dot(hraw[...], perm[...], preferred_element_type=F32).astype(BF16)
    for i in range(XS - 1):
        send_h(i).start()
    for q in range(1, NQ):
        for i in range(XS - 1):
            send_w(q, i).start()

    table = jnp.zeros((EXP, TOK), F32)
    pidx = iota((EXP, TOK), 1)
    for p in range(CAP):
        value = jnp.sum(jnp.where(qt == float(p), gate_t, 0.0), axis=1, keepdims=True)
        table = jnp.where(pidx == p, value, table)
    for i in range(ZS):
        gsend[i] = table[i * E8:(i + 1) * E8]
    grecv[z] = gsend[z]
    small_start(K_G, peers_z, lambda there: gsend.at[there], grecv, z)

    def build_sel():
        small_wait(K_Q, peers_z, qrecv)
        ridx = iota((GZ * CAP, TOK), 0).astype(F32)
        for g in range(ZS // GZ):
            for i in range(GZ):
                tile = qrecv[g * GZ + i]
                want = jnp.where(tile >= 0.0, tile + float(i * CAP), -1.0)
                for e in range(E8):
                    sel[g, e * GZ * CAP:(e + 1) * GZ * CAP, i * TOK:(i + 1) * TOK] = (
                        ridx == want[e:e + 1, :]).astype(F32).astype(BF16)

    def send_y(q, i):
        dev, there = out_y[i]
        return pltpu.make_async_remote_copy(
            src_ref=sendb.at[q, there], dst_ref=rows.at[q, blk(me8, BLK)],
            send_sem=ys.at[q, i], recv_sem=yr.at[q, me8], device_id=dev, device_id_type=MESH)

    def own_rows(q):
        return pltpu.make_async_copy(sendb.at[q, me8], rows.at[q, blk(me8, BLK)], loc.at[1 + 2 * NQ + q])

    def select(q):
        for g in range(ZS // GZ):
            got = jnp.dot(sel[g], tok[q, g * GZ * TOK:(g + 1) * GZ * TOK, :], preferred_element_type=F32).astype(BF16)
            for e in range(E8):
                sendb[q, e, g * GZ * CAP:(g + 1) * GZ * CAP, :] = got[e * GZ * CAP:(e + 1) * GZ * CAP]
        for i in range(E8 - 1):
            send_y(q, i).start()
        own_rows(q).start()

    for t in range(2, HALF + NQ + 1):
        for q in range(NQ):
            s = t - q
            if s == 1:
                get_t[q].wait()
            if 1 <= s <= HALF:
                ring_step(q, s)
            if s == HALF + 1:
                if q == 0:
                    build_sel()
                ring_end(q)
                select(q)
                if q == 0:
                    small_wait(K_G, peers_z, grecv)
                    for zz in range(ZS):
                        for e in range(E8):
                            gsy[e, zz:zz + 1, :] = grecv[zz, e:e + 1, :]
                    gtab[me8] = gsy[me8]
                    small_start(K_GY, out_y, lambda there: gsy.at[there], gtab, me8)

    small_wait(K_GY, out_y, gtab)
    spread = (iota((TOK, SLOTS), 0) == place).astype(F32).astype(BF16)
    gsrc = gtab[...].reshape(EXP, TOK).astype(BF16)
    gate_all = jnp.dot(gsrc, spread, preferred_element_type=F32)
    pick = iota((EXP, SLOTS), 0) == source
    gate_lane = jnp.sum(jnp.where(pick, gate_all, 0.0), axis=0, keepdims=True)
    for i in range(XS):
        if i > 0:
            dev, there = peers_x[i - 1]
            pltpu.make_async_remote_copy(
                src_ref=hx.at[blk(there, FFD)], dst_ref=hx.at[blk(there, FFD)], send_sem=hsn.at[0],
                recv_sem=hr.at[there], device_id=dev, device_id_type=MESH).wait_recv()
    for i in range(XS):
        part = slice(i * FFD, (i + 1) * FFD)
        hs[part, :] = (hx[part, :].astype(F32) * gate_lane).astype(BF16)
    for j in range(SLOTS // PB):
        hxt[j * PB:(j + 1) * PB, :] = hx[:, j * PB:(j + 1) * PB].T

    def wait_w(q):
        own_w(q).wait()
        for i in range(XS - 1):
            dev, there = peers_x[i]
            pltpu.make_async_remote_copy(
                src_ref=w_hbm.at[0, :, col(x * DX + q * DQ)], dst_ref=wv.at[q, blk(there, FFD)],
                send_sem=ws.at[q, 0], recv_sem=wr.at[q, there], device_id=dev, device_id_type=MESH).wait_recv()

    def wait_rows(q):
        own_rows(q).wait()
        for i in range(E8 - 1):
            dev, there = out_y[i]
            pltpu.make_async_remote_copy(
                src_ref=sendb.at[q, there], dst_ref=rows.at[q, blk(there, BLK)],
                send_sem=ys.at[q, 0], recv_sem=yr.at[q, there], device_id=dev, device_id_type=MESH).wait_recv()

    def send_o(q, i):
        dev, there = peers_x[i]
        return pltpu.make_async_remote_copy(
            src_ref=wgs.at[q, blk(there, FFD)], dst_ref=out_hbm.at[0, :, col(x * DX + q * DQ)],
            send_sem=osn.at[q, i], recv_sem=orc.at[q, x], device_id=dev, device_id_type=MESH)

    def own_o(q):
        return pltpu.make_async_copy(
            wgs.at[q, blk(x, FFD)], out_hbm.at[0, :, col(x * DX + q * DQ)], loc.at[1 + 3 * NQ + q])

    acc[...] = jnp.zeros_like(acc)
    order = [1, 0, 2, 3][:XS - 1] if XS == 4 else list(range(XS - 1))
    order = [i for i in order if i < XS - 1] + [None]

    def chunk(q, squares):
        wait_rows(q)
        for i in order:
            there = x if i is None else peers_x[i][1]
            wg = jnp.dot(hs[blk(there, FFD), :], rows[q], preferred_element_type=F32)
            wgs[q, blk(there, FFD), :] = wg.astype(BF16)
            if i is None:
                own_o(q).start()
            else:
                send_o(q, i).start()
            squares = squares + jnp.sum((wg * wg).reshape(FFD // 8, 8, DQ), axis=0)
        wait_w(q)
        gback = jnp.dot(hxt[...], wv[q], preferred_element_type=F32)
        both = gback * rows[q].astype(F32)
        for i in range(DQ // 128):
            acc[...] += both[:, i * 128:(i + 1) * 128]
        return squares

    squares = lax.fori_loop(0, NQ, chunk, jnp.zeros((8, DQ), F32))
    tile = squares[:, 0:128]
    for i in range(1, DQ // 128):
        tile = tile + squares[:, i * 128:(i + 1) * 128]

    pa[tp] = tile
    small_start(K_PA, peers_tp, lambda there: pa.at[tp], pa, tp)

    partial = jnp.sum(acc[...], axis=1, keepdims=True)
    place_t = place_col(SLOTS, CAP)
    by_place = jnp.where(iota((SLOTS, TOK), 1) == place_t, partial, 0.0)
    back = jnp.dot(pick.astype(F32), by_place, preferred_element_type=F32, precision=lax.Precision.HIGHEST)
    for e in range(E8):
        rsend[e] = back[e * ZS:(e + 1) * ZS]
    ry[me8] = rsend[me8]
    small_start(K_RY, back_y, lambda there: rsend.at[there], ry, me8)

    small_wait(K_PA, peers_tp, pa)
    pb[me8] = jnp.sum(pa[...], axis=0)
    small_start(K_PB, out_y, lambda there: pb.at[me8], pb, me8)

    small_wait(K_RY, out_y, ry)
    for zz in range(ZS):
        for e in range(E8):
            rzs[zz, e:e + 1, :] = ry[e, zz:zz + 1, :]
    rz[z] = rzs[z]
    small_start(K_RZ, peers_z, lambda there: rzs.at[there], rz, z)

    small_wait(K_PB, out_y, pb)
    pc[z] = jnp.sum(pb[...], axis=0)
    small_start(K_PC, peers_z, lambda there: pc.at[z], pc, z)

    small_wait(K_RZ, peers_z, rz)
    by_expert = rz[...].reshape(EXP, TOK)
    qt2 = qsend[...].reshape(EXP, TOK)
    value = jnp.zeros((EXP, TOK), F32)
    for p in range(CAP):
        value = jnp.where(qt2 == float(p), by_expert[:, p:p + 1], value)
    found = [
        jnp.sum(jnp.where(routes_ref[k:k + 1, :] == eidx, value, 0.0), axis=0, keepdims=True) for k in range(TOP)
    ]
    gg[tp] = jnp.concatenate(found, axis=0)
    small_start(K_GG, peers_tp, lambda there: gg.at[tp], gg, tp)

    small_wait(K_PC, peers_z, pc)
    total_ref[...] = jnp.sum(pc[...], axis=0)
    small_wait(K_GG, peers_tp, gg)
    gg_ref[...] = jnp.sum(gg[...], axis=0)

    for q in range(NQ):
        own_o(q).wait()
        for i in range(XS - 1):
            dev, there = peers_x[i]
            pltpu.make_async_remote_copy(
                src_ref=wgs.at[q, blk(there, FFD)], dst_ref=out_hbm.at[0, :, col(there * DX + q * DQ)],
                send_sem=osn.at[q, 0], recv_sem=orc.at[q, there], device_id=dev, device_id_type=MESH).wait_recv()
            send_o(q, i).wait_send()
            send_w(q, i).wait_send()
        for i in range(E8 - 1):
            send_y(q, i).wait_send()
    for i in range(XS - 1):
        send_h(i).wait_send()
    for d in sent:
        d.wait_send()
    small_done(K_Q, peers_z, lambda there: qsend.at[there], qrecv, z)
    small_done(K_G, peers_z, lambda there: gsend.at[there], grecv, z)
    small_done(K_GY, out_y, lambda there: gsy.at[there], gtab, me8)
    small_done(K_PA, peers_tp, lambda there: pa.at[tp], pa, tp)
    small_done(K_PB, out_y, lambda there: pb.at[me8], pb, me8)
    small_done(K_PC, peers_z, lambda there: pc.at[z], pc, z)
    small_done(K_RY, back_y, lambda there: rsend.at[there], ry, me8)
    small_done(K_RZ, peers_z, lambda there: rzs.at[there], rz, z)
    small_done(K_GG, peers_tp, lambda there: gg.at[tp], gg, tp)


def place_col(slots, cap):
    at = iota((slots, 1), 0).astype(F32) + 0.5
    return (at - jnp.floor(at * (1.0 / cap)) * cap - 0.5).astype(jnp.int32)


def per_device(grad_out, routes, gates, hidden, w_down):
    E8, TPS = CS * YS, XS * HS
    EXP = ZS * E8
    TOK, D = grad_out.shape
    TOP = routes.shape[1]
    FFD, SLOTS = hidden.shape[1], hidden.shape[2]
    DX = D // XS
    DQ = DX // NQ
    GZ = min(4, ZS)
    BLK = ZS * CAP
    vm = pltpu.VMEM
    dma = pltpu.SemaphoreType.DMA
    most = max(TPS, E8, ZS)
    any_space = pl.BlockSpec(memory_space=pl.ANY)
    in_vmem = pl.BlockSpec(memory_space=pltpu.VMEM)
    part, squares, gate_grad = pl.pallas_call(
        kernel,
        out_shape=(
            jax.ShapeDtypeStruct((1, FFD, D), BF16),
            jax.ShapeDtypeStruct((8, 128), F32),
            jax.ShapeDtypeStruct((TOP, TOK), F32),
        ),
        in_specs=[in_vmem, in_vmem, any_space, any_space, any_space],
        out_specs=(any_space, in_vmem, in_vmem),
        scratch_shapes=[
            vm((NQ, ZS * TOK, DQ), BF16),
            vm((ZS // GZ, E8 * GZ * CAP, GZ * TOK), BF16),
            vm((NQ, E8, BLK, DQ), BF16),
            vm((NQ, SLOTS, DQ), BF16),
            vm((ZS, E8, TOK), F32),
            vm((ZS, E8, TOK), F32),
            vm((ZS, E8, TOK), F32),
            vm((ZS, E8, TOK), F32),
            vm((E8, ZS, TOK), F32),
            vm((E8, ZS, TOK), F32),
            vm((FFD, SLOTS), BF16),
            vm((SLOTS, SLOTS), BF16),
            vm((XS * FFD, SLOTS), BF16),
            vm((XS * FFD, SLOTS), BF16),
            vm((SLOTS, XS * FFD), BF16),
            vm((NQ, XS * FFD, DQ), BF16),
            vm((NQ, XS * FFD, DQ), BF16),
            vm((SLOTS, 128), F32),
            vm((TPS, 8, 128), F32),
            vm((E8, 8, 128), F32),
            vm((ZS, 8, 128), F32),
            vm((E8, ZS, TOK), F32),
            vm((E8, ZS, TOK), F32),
            vm((ZS, E8, TOK), F32),
            vm((ZS, E8, TOK), F32),
            vm((TPS, TOP, TOK), F32),
            dma((1 + 4 * NQ,)),
            dma((NQ, ZS)),
            dma((NQ, ZS)),
            dma((NQ, E8)),
            dma((NQ, E8)),
            dma((NQ, XS)),
            dma((NQ, XS)),
            dma((XS,)),
            dma((XS,)),
            dma((NQ, XS)),
            dma((NQ, XS)),
            dma((9, most)),
            dma((9, most)),
        ],
        compiler_params=pltpu.CompilerParams(
            collective_id=0, has_side_effects=True, vmem_limit_bytes=56 * 1024 * 1024),
        cost_estimate=pl.CostEstimate(
            flops=2 * 2 * SLOTS * FFD * D, bytes_accessed=8 * 1024 * 1024, transcendentals=0),
        name="moe_down_backward",
    )(routes.T, gates.T, grad_out, hidden, w_down)
    entries = FFD * D * TPS * EXP
    clip_limit = clip_ratio * math.sqrt(entries)
    factor = jnp.minimum(1.0, clip_limit / (jnp.sqrt(jnp.sum(squares)) + 1e-06))
    down_grad = (part.astype(F32) * factor).astype(BF16)
    return (down_grad, gate_grad.T)


def solution(mesh):
    in_specs = (
        P(("dp", "edp"), None),
        P(("dp", "edp"), None),
        P(("dp", "edp"), None),
        P(("dp", "edp"), "tp", None),
        P(("dp", "edp"), "tp", None),
    )
    out_specs = (P(("dp", "edp"), "tp", None), P(("dp", "edp"), None))
    return jax.shard_map(
        per_device, mesh=mesh, in_specs=in_specs, out_specs=out_specs, check_vma=False
    )
```

time: 712 us -> 92.6 us (0.13)
  waiting for transfers between devices: 333 us -> 0 us
  blocking collectives: 223 us -> 0 us
  Pallas kernels: 0 us -> 85.4 us
  local copies, waits for them, and re-layouts: 64.6 us -> 0.6 us
  starting transfers between devices: 33.4 us -> 0 us
  other arithmetic: 33.8 us -> 4.14 us
  matrix products: 16 us -> 0 us
    all_to_all x3 -> x0, waiting for transfers between devices: 333 us -> none  [the longest x1 327 us: per_device(): lax.all_to_all(outgoing, ('dp', 'edp'), split_axis=0, concat_axis=0, tile...]
    psum x2 -> x0, blocking collectives: 223 us -> none  [the longest x1 179 us: per_device(): total_squares = lax.psum(squares, ('tp', 'dp', 'edp'))]
    pallas_call x0 -> x1, Pallas kernels: none -> 85.4 us  [per_device(): pl.pallas_call(kernel, out_shape=(jax.ShapeDtypeStruct((1, FFD, D), BF16)...]
    gather x4 -> x0, local copies, waits for them, and re-layouts: 36.3 us -> none  [the longest x2 22.2 us: per_device(): grad_out[tokens_of] * slot_live[:, None]]
    all_to_all x3 -> x0, starting transfers between devices: 33.4 us -> none  [the longest x1 15.4 us: per_device(): lax.all_to_all(gate_slots, ('dp', 'edp'), split_axis=0, concat_axis=0, ti...]
    another operation x3 -> x0, other arithmetic: 18.2 us -> none
    dot_general x2 -> x0, matrix products: 16 us -> none  [the longest x1 8.46 us: dense_products(): weight_grad = jnp.dot(scaled, row_block, preferred_element_type=jnp.float32)]
    reshape x4 -> x0, local copies, waits for them, and re-layouts: 14.3 us -> none  [the longest x1 14 us: per_device(): row_block = arrived.reshape(slot_total, model_width)]
  transfers between devices with their start and end apart: 3 -> 0, of which waited for: 2 -> 0; matrix products, arithmetic and copies ran while one was open for 5% -> 0% of each run, Pallas kernels for 0% -> 0%
where the time goes in v1:
time: 92.6 us; the launch traced here: 91.5 us
  Pallas kernels  85.4 us (92%)
  other arithmetic  4.14 us (4%)
  between operations  1.38 us (1%)
    pallas_call x1, Pallas kernels, per_device(): pl.pallas_call(kernel, out_shape=(jax.ShapeDtypeStruct((1, FFD, D), BF16)...  85.4 us
    convert_element_type x1, other arithmetic, per_device(): down_grad = (part.astype(F32) * factor).astype(BF16)  2.86 us

profile of v1, /device:TPU:1, one launch (start us, length us, event | category | flops | bytes accessed | tf_op | source)
XLA Modules:
  0.0 91.5 jit_solution(9709644696662142153)
XLA Ops:
  0.6 85.4 %moe_down_backward.1 = (bf16[1,192,4096]{2,1,0:T(8,128)(2,1)}, f32[8,128]{1,0:T(8,128)}, f32[8,128]{1,0:T(8,128)}) custom-call(s32[8,128]{1,0:T(8,128)} %bitcast.4, bf16[8,128]{1,0:T(8,128)(2,1)} %bitcast.5, bf16[128,4096]{1,0:T(8,128)(2,1)} %grad_hbm.1, bf16[1,192,1280]{2,1,0:T(8,128)(2,1)} %hid_hbm.1, bf16[1,192,4096]{2,1,0:T(8,128)(2,1)} %w_hbm.1), custom_call_target="tpu_custom_call" | custom-call | flops 4026531840 | bytes 8388608 | tf_op jit(solution)/shard_map/moe_down_backward/pallas_call | solution.py:435
  86.0 1.3 %reduce_sum.9 = f32[]{:T(128)} reduce(f32[8,128]{1,0:T(8,128)} %get-tuple-element.6, f32[]{:T(128)} %constant.1.clone.1), dimensions={0,1}, to_apply=%region_0.0 | reduce | flops 1023 | bytes 4104 | tf_op jit(solution)/shard_map/reduce_sum | solution.py:493
  88.0 0.0 copy-start
  88.0 2.9 %multiply_convert_fusion = bf16[1,192,4096]{2,1,0:T(8,128)(2,1)} fusion(bf16[1,192,4096]{2,1,0:T(8,128)(2,1)} %get-tuple-element.5, f32[]{:T(128)S(6)} %min_shard_map.3), kind=kLoop, calls=%fused_computation | loop fusion | flops 2359296 | bytes 3145732 | tf_op jit(solution)/shard_map/convert_element_type | solution.py:494
  90.9 0.0 copy-done
  90.9 0.6 copy.8
Async XLA Ops:
  88.0 2.9 %copy-start = (f32[8,128]{1,0:T(8,128)S(1)}, f32[8,128]{1,0:T(8,128)}, u32[]{:S(2)}) copy-start(f32[8,128]{1,0:T(8,128)} %get-tuple-element.7) | copy-start | bytes 12292

commit v2 on v0

v2 whole, which is shorter than its diff:
```python
import functools
import math

import jax
import jax.numpy as jnp
from jax import lax
from jax.experimental import pallas as pl
from jax.experimental.pallas import tpu as pltpu
from jax.sharding import PartitionSpec as P

clip_ratio = 0.25

XS, HS, ZS, CS, YS = 4, 2, 8, 2, 4
NQ = 2
NR = 4
CAP = 20
AWAY = {8: [0, 1, -1, -2, 2, 3, -3, 4], 4: [0, 1, -1, 2], 2: [0, 1]}
MESH = pl.DeviceIdType.MESH
F32, BF16 = jnp.float32, jnp.bfloat16


def slot_groups():
    whole = CAP // 16 * 16
    rest = lambda parts: [(r, whole, CAP) for r in parts if CAP > whole]
    head = lambda parts: [(r, 0, whole) for r in parts]
    if ZS == 8:
        return [head([0, 1, 2]), head([3, 4]) + rest([0, 1, 2, 3]), head([5, 6]), head([7]) + rest([4, 5, 6, 7])]
    if ZS == 4:
        return [head([0, 1, 2]), head([3]) + rest([0, 1, 2, 3])]
    return [head([0, 1]) + rest([0, 1])]


K_Q, K_GY, K_RY, K_RZ, K_GG = range(5)


def iota(shape, dim):
    return lax.broadcasted_iota(jnp.int32, shape, dim)


def kernel(
    routes_hbm, gates_hbm, grad_hbm, hid_hbm, w_hbm,
    out_hbm, factor_ref, gg_ref,
    routes_ref, gates_ref, tok, sel, sendb, rows, qsend, qrecv, gsy, gtab,
    hraw, perm, hx, hs, hxt, wv, wgs, gbk, acc, bp, spread_t, rsend, ry, rzs, rz, gg,
    loc, zs, zr, ys, yr, ws, wr, hsn, hr, hfs, hfr, osn, orc, sms, smr,
):
    E8 = CS * YS
    TPS = XS * HS
    EXP = ZS * E8
    TOK, TOP = routes_ref.shape[1], routes_ref.shape[0]
    FFD = hid_hbm.shape[1]
    SLOTS = hid_hbm.shape[2]
    D = w_hbm.shape[2]
    DX = D // XS
    DQ = DX // NQ
    DR = DX // NR
    BLK = ZS * CAP
    HALF = ZS // 2
    away = AWAY[ZS]
    groups = slot_groups()
    GROUPS = len(groups)
    sizes = [sum(b - a for _, a, b in g) for g in groups]
    firsts = [sum(sizes[:i]) for i in range(GROUPS)]
    spans = [(min(r for r, _, _ in g), max(r for r, _, _ in g) + 1) for g in groups]

    def slot(d):
        return away.index(d + ZS if d <= -HALF else d)

    tp = lax.axis_index("tp")
    dp = lax.axis_index("dp")
    y = lax.axis_index("edp")
    x, h = lax.div(tp, HS), lax.rem(tp, HS)
    z, c = lax.div(dp, CS), lax.rem(dp, CS)
    yy = h * YS + y
    me8 = c * YS + y

    def at_y(delta, core):
        there = lax.rem(yy + delta + HS * YS, HS * YS)
        ylo = lax.rem(there, YS)
        return (x * HS + lax.div(there, YS), z * CS + core, ylo), core * YS + ylo

    def at_z(delta):
        zz = lax.rem(z + delta + ZS, ZS)
        return (tp, zz * CS + c, y), zz

    def at_x(delta):
        xx = lax.rem(x + delta, XS)
        return (xx * HS + h, dp, y), xx

    out_y = [at_y(2, 0), at_y(-2, 1), at_y(1, 0), at_y(-1, 0), at_y(1, 1), at_y(-1, 1), at_y(0, 1 - c)]
    all_y = [at_y(delta, core) for delta in (4, 3, -3, 2, -2, 1, -1) for core in range(CS)] + [at_y(0, 1 - c)]
    peers_z = [at_z(away[r]) for r in range(ZS - 1, 0, -1)]
    slots_z = list(range(ZS - 1, 0, -1))
    peers_x = [at_x(i) for i in ((2, 1, 3) if XS == 4 else range(1, XS))]
    near_x = [i for i in range(XS - 1) if XS < 4 or i > 0]

    barrier = pltpu.get_barrier_semaphore()
    hello = [d for d, _ in peers_z] + [d for d, _ in peers_x] + [d for d, _ in all_y]
    for d in hello:
        pl.semaphore_signal(barrier, inc=1, device_id=d, device_id_type=MESH)

    def col(start, size):
        return pl.ds(pl.multiple_of(start, size), size)

    def blk(start, size):
        return pl.ds(pl.multiple_of(start * size, size), size)

    get_r = pltpu.make_async_copy(routes_hbm, routes_ref, loc.at[1 + NR + 2 * NQ + NQ * GROUPS])
    get_r.start()
    get_g = pltpu.make_async_copy(gates_hbm, gates_ref, loc.at[2 + NR + 2 * NQ + NQ * GROUPS])
    get_g.start()
    get_t = [
        pltpu.make_async_copy(grad_hbm.at[:, col(x * DX + p * DR, DR)], tok.at[p, 0:TOK], loc.at[1 + p])
        for p in range(NR)
    ]
    for d in get_t:
        d.start()
    get_h = pltpu.make_async_copy(hid_hbm.at[0], hraw, loc.at[0])
    get_h.start()

    def own_w(q):
        return pltpu.make_async_copy(
            w_hbm.at[0, :, col(x * DX + q * DQ, DQ)], wv.at[q, blk(x, FFD)], loc.at[1 + NR + q])

    for q in range(NQ):
        own_w(q).start()

    get_r.wait()
    get_g.wait()
    eidx = iota((EXP, TOK), 0)
    chosen = jnp.zeros((EXP, TOK), F32)
    gate_t = jnp.zeros((EXP, TOK), F32)
    gates_f = gates_ref[...].astype(F32)
    for k in range(TOP):
        hit = routes_ref[k:k + 1, :] == eidx
        chosen = jnp.where(hit, 1.0, chosen)
        gate_t = jnp.where(hit, gates_f[k:k + 1, :], gate_t)
    earlier = (iota((TOK, TOK), 0) < iota((TOK, TOK), 1)).astype(F32).astype(BF16)
    count = jnp.dot(chosen.astype(BF16), earlier, preferred_element_type=F32)
    qt = jnp.where(chosen > 0.5, count, -1.0)
    table = jnp.zeros((EXP, TOK), F32)
    pidx = iota((EXP, TOK), 1)
    for p in range(CAP):
        value = jnp.sum(jnp.where(qt == float(p), gate_t, 0.0), axis=1, keepdims=True)
        table = jnp.where(pidx == p, value, table)
    for i in range(ZS):
        qsend[i, 0:E8] = qt[i * E8:(i + 1) * E8]
        qsend[i, E8:2 * E8] = table[i * E8:(i + 1) * E8]
    qrecv[0] = qsend[z]

    lane = (iota((1, SLOTS), 1).astype(F32) + 0.5)
    group = jnp.floor(lane * (1.0 / BLK))
    inner = (lane - group * BLK).astype(jnp.int32)
    group = group.astype(jnp.int32)
    part_z = jnp.zeros((1, SLOTS), jnp.int32)
    from_z = jnp.zeros((1, SLOTS), jnp.int32)
    place = jnp.zeros((1, SLOTS), jnp.int32)
    start = 0
    for r, a, b in [seg for g in groups for seg in g]:
        here = (inner >= start) & (inner < start + b - a)
        part_z = jnp.where(here, r, part_z)
        from_z = jnp.where(here, lax.rem(z + away[r] + ZS, ZS), from_z)
        place = jnp.where(here, inner - (start - a), place)
        start += b - a
    source = group * ZS + part_z
    native = from_z * (E8 * CAP) + group * CAP + place

    PB = 128

    def build_perm(i, carry):
        perm[pl.ds(pl.multiple_of(i * PB, PB), PB), :] = (
            (iota((PB, SLOTS), 0) + i * PB) == native).astype(F32).astype(BF16)
        return carry

    lax.fori_loop(0, SLOTS // PB, build_perm, 0)

    get_h.wait()
    hx[blk(x, FFD), :] = jnp.dot(hraw[...], perm[...], preferred_element_type=F32).astype(BF16)

    pl.semaphore_wait(barrier, len(hello))

    def remote(src, dst, send_sem, recv_sem, dev):
        return pltpu.make_async_remote_copy(
            src_ref=src, dst_ref=dst, send_sem=send_sem, recv_sem=recv_sem, device_id=dev, device_id_type=MESH)

    waited = set()

    def have(p, d):
        r = slot(d)
        if r > 0 and (p, r) not in waited:
            waited.add((p, r))
            part = tok.at[p, r * TOK:(r + 1) * TOK]
            remote(part, part, zs.at[p, 0], zr.at[p, r], peers_z[-1][0]).wait_recv()

    sent = []

    def ring(s, pieces):
        for p in pieces:
            if s > HALF:
                continue
            for right in ([True, False] if s < HALF else [p % 2 == 0]):
                d = -(s - 1) if right else s - 1
                have(p, d)
                to = slot(d - 1 if right else d + 1)
                a = slot(d)
                dev = at_z(1 if right else -1)[0]
                copy = remote(
                    tok.at[p, a * TOK:(a + 1) * TOK], tok.at[p, to * TOK:(to + 1) * TOK],
                    zs.at[p, to], zr.at[p, to], dev)
                copy.start()
                sent.append(copy)

    def q_copy(i):
        dev, there = peers_z[i]
        r = slot(-away[slots_z[i]])
        return remote(qsend.at[there], qrecv.at[r], sms.at[K_Q, i], smr.at[K_Q, r], dev)

    def send_w(q, i):
        dev, there = peers_x[i]
        return remote(
            w_hbm.at[0, :, col(there * DX + q * DQ, DQ)], wv.at[q, blk(x, FFD)], ws.at[q, i], wr.at[q, x], dev)

    def send_h(i):
        dev, there = peers_x[i]
        part = hx.at[blk(x, FFD)]
        return remote(part, part, hsn.at[i], hr.at[x], dev)

    pieces = list(range(NR))
    for p in pieces[:NR // 2]:
        get_t[p].wait()
    ring(1, pieces[:NR // 2])
    for i in range(ZS - 1):
        q_copy(i).start()
    for i in near_x:
        send_h(i).start()
    for p in pieces[NR // 2:]:
        get_t[p].wait()
    ring(1, pieces[NR // 2:])
    for i in near_x:
        send_w(0, i).start()

    def got_h(i):
        dev, there = peers_x[i]
        part = hx.at[blk(there, FFD)]
        remote(part, part, hsn.at[0], hr.at[there], dev).wait_recv()

    def pass_h(i):
        frm = peers_x[1 if i == 1 else 2][1]
        part = hx.at[pl.ds(pl.multiple_of(frm * FFD + i * (FFD // 2), FFD // 2), FFD // 2)]
        return remote(part, part, hfs.at[i], hfr.at[i], peers_x[2 if i == 1 else 1][0])

    def more_x():
        if XS == 4:
            for i in range(2):
                got_h(2 - i)
                pass_h(i).start()
            send_w(0, 0).start()
        for q in range(1, NQ):
            for i in range(XS - 1):
                send_w(q, i).start()

    heard = set()

    def build_sel(g):
        if g >= GROUPS:
            return
        lo, hi = spans[g]
        n = sizes[g]
        at = iota((n, TOK), 0)
        for r in range(lo, hi):
            if r > 0 and r not in heard:
                heard.add(r)
                remote(qsend.at[0], qrecv.at[r], sms.at[K_Q, 0], smr.at[K_Q, r], peers_z[0][0]).wait_recv()
            want = jnp.full((n, TOK), -7, jnp.int32)
            start = 0
            for rr, a, b in groups[g]:
                if rr == r:
                    want = jnp.where((at >= start) & (at < start + b - a), at - (start - a), want)
                start += b - a
            want = want.astype(F32)
            tile = qrecv[r, 0:E8]
            for e in range(E8):
                sel[g][e * n:(e + 1) * n, (r - lo) * TOK:(r - lo + 1) * TOK] = (
                    want == tile[e:e + 1, :]).astype(F32).astype(BF16)

    def part_of(expert, g):
        return pl.ds(pl.multiple_of(expert * BLK + firsts[g], 16), sizes[g])

    def send_y(q, g, i):
        dev, there = out_y[i]
        return remote(
            sendb.at[q, there, firsts[g]:firsts[g] + sizes[g]], rows.at[q, part_of(me8, g)],
            ys.at[q, g, i], yr.at[q, g, me8], dev)

    def own_rows(q, g):
        return pltpu.make_async_copy(
            sendb.at[q, me8, firsts[g]:firsts[g] + sizes[g]], rows.at[q, part_of(me8, g)],
            loc.at[1 + NR + NQ + q * GROUPS + g])

    def select(q, g):
        if g >= GROUPS:
            return
        lo, hi = spans[g]
        n = sizes[g]
        for p in range(q * NR // NQ, (q + 1) * NR // NQ):
            for r in range(lo, hi):
                have(p, away[r])
            got = jnp.dot(sel[g][...], tok[p, lo * TOK:hi * TOK, :], preferred_element_type=F32).astype(BF16)
            at = (p - q * NR // NQ) * DR
            for e in range(E8):
                sendb[q, e, firsts[g]:firsts[g] + n, at:at + DR] = got[e * n:(e + 1) * n]
        for i in range(E8 - 1):
            send_y(q, g, i).start()
        own_rows(q, g).start()

    def gy_copy(i):
        dev, there = out_y[i]
        return remote(gsy.at[there], gtab.at[me8], sms.at[K_GY, i], smr.at[K_GY, me8], dev)

    def gates_on():
        for r in range(1, ZS):
            if r not in heard:
                heard.add(r)
                remote(qsend.at[0], qrecv.at[r], sms.at[K_Q, 0], smr.at[K_Q, r], peers_z[0][0]).wait_recv()
        for r in range(ZS):
            for e in range(E8):
                gsy[e, r:r + 1, :] = qrecv[r, E8 + e:E8 + e + 1, :]
        gtab[me8] = gsy[me8]
        for i in range(E8 - 1):
            gy_copy(i).start()

    first, second = pieces[:NR // 2], pieces[NR // 2:]
    ring(2, first)
    build_sel(0)
    select(0, 0)
    ring(2, second)
    select(1, 0)
    ring(3, first)
    build_sel(1)
    select(0, 1)
    ring(3, second)
    select(1, 1)
    build_sel(2)
    gates_on()
    ring(4, first)
    select(0, 2)
    more_x()
    build_sel(3)
    ring(4, second)
    select(1, 2)
    select(0, 3)
    select(1, 3)

    if XS == 4:
        for i in range(2):
            part = hx.at[pl.ds(pl.multiple_of(peers_x[0][1] * FFD + i * (FFD // 2), FFD // 2), FFD // 2)]
            remote(part, part, hfs.at[i], hfr.at[i], peers_x[1][0]).wait_recv()
    else:
        for i in near_x:
            got_h(i)
    for j in range(SLOTS // PB):
        hxt[j * PB:(j + 1) * PB, :] = hx[:, j * PB:(j + 1) * PB].T
    for dev, there in out_y:
        remote(gsy.at[there], gtab.at[there], sms.at[K_GY, 0], smr.at[K_GY, there], dev).wait_recv()
    spread = (iota((TOK, SLOTS), 0) == place).astype(F32)
    for j in range(SLOTS // PB):
        spread_t[j * PB:(j + 1) * PB, :] = spread[:, j * PB:(j + 1) * PB].T
    spread = spread.astype(BF16)
    gate_all = jnp.dot(gtab[...].reshape(EXP, TOK).astype(BF16), spread, preferred_element_type=F32)
    pick = iota((EXP, SLOTS), 0) == source
    gate_lane = jnp.sum(jnp.where(pick, gate_all, 0.0), axis=0, keepdims=True)
    for i in range(XS):
        part = slice(i * FFD, (i + 1) * FFD)
        hs[part, :] = (hx[part, :].astype(F32) * gate_lane).astype(BF16)

    def wait_w(q):
        own_w(q).wait()
        for dev, there in peers_x:
            remote(
                w_hbm.at[0, :, col(x * DX + q * DQ, DQ)], wv.at[q, blk(there, FFD)],
                ws.at[q, 0], wr.at[q, there], dev).wait_recv()

    def wait_rows(q):
        for g in range(GROUPS):
            own_rows(q, g).wait()
            for dev, there in out_y:
                remote(
                    sendb.at[q, there, firsts[g]:firsts[g] + sizes[g]], rows.at[q, part_of(there, g)],
                    ys.at[q, g, 0], yr.at[q, g, there], dev).wait_recv()

    def send_o(q, i):
        dev, there = peers_x[i]
        return remote(
            wgs.at[q, blk(there, FFD)], out_hbm.at[0, :, col(x * DX + q * DQ, DQ)],
            osn.at[q, i], orc.at[q, x], dev)

    def own_o(q):
        return pltpu.make_async_copy(
            wgs.at[q, blk(x, FFD)], out_hbm.at[0, :, col(x * DX + q * DQ, DQ)],
            loc.at[1 + NR + NQ + NQ * GROUPS + q])

    def products(q, squares):
        wait_rows(q)
        for i in range(XS):
            there = x if i == XS - 1 else peers_x[i][1]
            wg = jnp.dot(hs[blk(there, FFD), :], rows[q], preferred_element_type=F32)
            wgs[q, blk(there, FFD), :] = wg.astype(BF16)
            if i == XS - 1:
                own_o(q).start()
            else:
                send_o(q, i).start()
            squares = squares + jnp.sum((wg * wg).reshape(FFD // 8, 8, DQ), axis=0)
        return squares

    def turned(q):
        wait_w(q)

        def body(j, carry):
            at = pl.ds(pl.multiple_of(j * PB, PB), PB)
            gbk[q, at, :] = jnp.dot(hxt[at, :], wv[q], preferred_element_type=F32)
            return carry

        lax.fori_loop(0, SLOTS // PB, body, 0)

    def fold(q, at):
        both = gbk[q, at, :] * rows[q, at, :].astype(F32)
        total = both[:, 0:128]
        for i in range(1, DQ // 128):
            total = total + both[:, i * 128:(i + 1) * 128]
        return total

    turned(0)
    squares = products(0, jnp.zeros((8, DQ), F32))

    def fold_first(j, carry):
        at = pl.ds(pl.multiple_of(j * PB, PB), PB)
        acc[at, :] = fold(0, at)
        return carry

    lax.fori_loop(0, SLOTS // PB, fold_first, 0)
    for q in range(1, NQ):
        squares = products(q, squares)
        turned(q)

    def fold_last(j, carry):
        at = pl.ds(pl.multiple_of(j * PB, PB), PB)
        total = acc[at, :]
        for q in range(1, NQ):
            total = total + fold(q, at)
        bp[at, :] = spread_t[at, :] * jnp.sum(total, axis=1, keepdims=True)
        return carry

    lax.fori_loop(0, SLOTS // PB, fold_last, 0)
    tile = squares[:, 0:128]
    for i in range(1, DQ // 128):
        tile = tile + squares[:, i * 128:(i + 1) * 128]

    back = jnp.dot(pick.astype(F32), bp[...], preferred_element_type=F32, precision=lax.Precision.HIGHEST)
    for e in range(E8):
        rsend[e, 0:ZS] = back[e * ZS:(e + 1) * ZS]
        rsend[e, ZS:ZS + 8] = tile

    def ry_copy(i):
        dev, there = all_y[i]
        return remote(rsend.at[there], ry.at[h * E8 + me8], sms.at[K_RY, i], smr.at[K_RY, h * E8 + me8], dev)

    def rz_copy(i):
        dev, there = peers_z[i]
        return remote(rzs.at[slots_z[i]], rz.at[z], sms.at[K_RZ, i], smr.at[K_RZ, z], dev)

    def gg_copy(i):
        dev, there = peers_x[i]
        return remote(gg.at[x], gg.at[x], sms.at[K_GG, i], smr.at[K_GG, x], dev)

    for i in range(len(all_y)):
        ry_copy(i).start()
    ry[h * E8 + me8] = rsend[me8]

    for q in range(NQ):
        for i in range(XS - 1):
            send_w(q, i).wait_send()
        for g in range(GROUPS):
            for i in range(E8 - 1):
                send_y(q, g, i).wait_send()
    for i in near_x:
        send_h(i).wait_send()
    if XS == 4:
        for i in range(2):
            pass_h(i).wait_send()
    for copy in sent:
        copy.wait_send()
    for i in range(ZS - 1):
        q_copy(i).wait_send()
    for i in range(E8 - 1):
        gy_copy(i).wait_send()

    for dev, there in all_y:
        there = lax.rem(dev[0], HS) * E8 + there
        remote(rsend.at[0], ry.at[there], sms.at[K_RY, 0], smr.at[K_RY, there], dev).wait_recv()

    tile = jnp.sum(ry[:, ZS:ZS + 8, :], axis=0)
    for r in range(ZS):
        for e in range(E8):
            rzs[r, e:e + 1, :] = ry[e, r:r + 1, :] + ry[E8 + e, r:r + 1, :]
        rzs[r, E8:E8 + 8] = tile
    for i in range(ZS - 1):
        rz_copy(i).start()
    rz[z] = rzs[0]
    for dev, there in peers_z:
        remote(rzs.at[0], rz.at[there], sms.at[K_RZ, 0], smr.at[K_RZ, there], dev).wait_recv()

    by_expert = rz[:, 0:E8, :].reshape(EXP, TOK)
    qt2 = qsend[:, 0:E8, :].reshape(EXP, TOK)
    value = jnp.zeros((EXP, TOK), F32)
    for p in range(CAP):
        value = jnp.where(qt2 == float(p), by_expert[:, p:p + 1], value)
    for k in range(TOP):
        gg[x, k:k + 1, :] = jnp.sum(
            jnp.where(routes_ref[k:k + 1, :] == eidx, value, 0.0), axis=0, keepdims=True)
    gg[x, 8:16, :] = jnp.sum(rz[:, E8:E8 + 8, :], axis=0)
    for i in range(XS - 1):
        gg_copy(i).start()
    for dev, there in peers_x:
        remote(gg.at[x], gg.at[there], sms.at[K_GG, 0], smr.at[K_GG, there], dev).wait_recv()

    total = jnp.sum(gg[:, 8:16, :], axis=0)
    total = jnp.sum(jnp.sum(total, axis=1, keepdims=True), axis=0, keepdims=True)
    limit = clip_ratio * math.sqrt(FFD * D * TPS * EXP)
    factor = jnp.minimum(1.0, limit / (jnp.sqrt(total) + 1e-06))
    factor_ref[...] = factor
    gg_ref[...] = jnp.sum(gg[:, 0:TOP, :], axis=0)

    for q in range(NQ):
        own_o(q).wait()
        for i in range(XS - 1):
            dev, there = peers_x[i]
            remote(
                wgs.at[q, blk(there, FFD)], out_hbm.at[0, :, col(there * DX + q * DQ, DQ)],
                osn.at[q, 0], orc.at[q, there], dev).wait_recv()
            send_o(q, i).wait_send()
    for i in range(ZS - 1):
        rz_copy(i).wait_send()
    for i in range(len(all_y)):
        ry_copy(i).wait_send()
    for i in range(XS - 1):
        gg_copy(i).wait_send()


def per_device(grad_out, routes, gates, hidden, w_down):
    E8, TPS = CS * YS, XS * HS
    TOK, D = grad_out.shape
    TOP = routes.shape[1]
    FFD, SLOTS = hidden.shape[1], hidden.shape[2]
    DX = D // XS
    DQ, DR = DX // NQ, DX // NR
    groups = slot_groups()
    GROUPS = len(groups)
    sizes = [sum(b - a for _, a, b in g) for g in groups]
    reach = [max(r for r, _, _ in g) + 1 - min(r for r, _, _ in g) for g in groups]
    vm = pltpu.VMEM
    dma = pltpu.SemaphoreType.DMA
    most = max(TPS, HS * E8, ZS)
    any_space = pl.BlockSpec(memory_space=pl.ANY)
    in_hbm = pl.BlockSpec(memory_space=pltpu.HBM)
    in_vmem = pl.BlockSpec(memory_space=pltpu.VMEM)
    part, factor, gate_grad = pl.pallas_call(
        kernel,
        out_shape=(
            jax.ShapeDtypeStruct((1, FFD, D), BF16),
            jax.ShapeDtypeStruct((1, 1), F32),
            jax.ShapeDtypeStruct((TOP, TOK), F32),
        ),
        in_specs=[in_hbm] * 5,
        out_specs=(any_space, in_vmem, in_vmem),
        scratch_shapes=[
            vm((TOP, TOK), jnp.int32),
            vm((TOP, TOK), BF16),
            vm((NR, ZS * TOK, DR), BF16),
            [vm((E8 * n, k * TOK), BF16) for n, k in zip(sizes, reach)],
            vm((NQ, E8, ZS * CAP, DQ), BF16),
            vm((NQ, SLOTS, DQ), BF16),
            vm((ZS, 2 * E8, TOK), F32),
            vm((ZS, 2 * E8, TOK), F32),
            vm((E8, ZS, TOK), F32),
            vm((E8, ZS, TOK), F32),
            vm((FFD, SLOTS), BF16),
            vm((SLOTS, SLOTS), BF16),
            vm((XS * FFD, SLOTS), BF16),
            vm((XS * FFD, SLOTS), BF16),
            vm((SLOTS, XS * FFD), BF16),
            vm((NQ, XS * FFD, DQ), BF16),
            vm((NQ, XS * FFD, DQ), BF16),
            vm((NQ, SLOTS, DQ), F32),
            vm((SLOTS, 128), F32),
            vm((SLOTS, TOK), F32),
            vm((SLOTS, TOK), F32),
            vm((E8, ZS + 8, TOK), F32),
            vm((HS * E8, ZS + 8, TOK), F32),
            vm((ZS, E8 + 8, TOK), F32),
            vm((ZS, E8 + 8, TOK), F32),
            vm((XS, 16, TOK), F32),
            dma((3 + NR + 2 * NQ + NQ * GROUPS,)),
            dma((NR, ZS)),
            dma((NR, ZS)),
            dma((NQ, GROUPS, E8)),
            dma((NQ, GROUPS, E8)),
            dma((NQ, XS)),
            dma((NQ, XS)),
            dma((XS,)),
            dma((XS,)),
            dma((2,)),
            dma((2,)),
            dma((NQ, XS)),
            dma((NQ, XS)),
            dma((5, most)),
            dma((5, most)),
        ],
        compiler_params=pltpu.CompilerParams(
            collective_id=0, has_side_effects=True, vmem_limit_bytes=40 * 1024 * 1024),
        cost_estimate=pl.CostEstimate(
            flops=2 * 2 * SLOTS * FFD * D, bytes_accessed=8 * 1024 * 1024, transcendentals=0),
        name="moe_down_backward",
    )(*[pltpu.with_memory_space_constraint(a, pltpu.HBM) for a in (routes.T, gates.T, grad_out, hidden, w_down)])
    down_grad = (part.astype(F32) * factor[0, 0]).astype(BF16)
    return (down_grad, gate_grad.T)


def solution(mesh):
    in_specs = (
        P(("dp", "edp"), None),
        P(("dp", "edp"), None),
        P(("dp", "edp"), None),
        P(("dp", "edp"), "tp", None),
        P(("dp", "edp"), "tp", None),
    )
    out_specs = (P(("dp", "edp"), "tp", None), P(("dp", "edp"), None))
    return jax.shard_map(
        per_device, mesh=mesh, in_specs=in_specs, out_specs=out_specs, check_vma=False
    )
```

time: 712 us -> 81.9 us (0.12)
  waiting for transfers between devices: 333 us -> 0 us
  blocking collectives: 223 us -> 0 us
  Pallas kernels: 0 us -> 78.5 us
  local copies, waits for them, and re-layouts: 64.6 us -> 0.59 us
  starting transfers between devices: 33.4 us -> 0 us
  other arithmetic: 33.8 us -> 2.01 us
  matrix products: 16 us -> 0 us
    all_to_all x3 -> x0, waiting for transfers between devices: 333 us -> none  [the longest x1 327 us: per_device(): lax.all_to_all(outgoing, ('dp', 'edp'), split_axis=0, concat_axis=0, tile...]
    psum x2 -> x0, blocking collectives: 223 us -> none  [the longest x1 179 us: per_device(): total_squares = lax.psum(squares, ('tp', 'dp', 'edp'))]
    pallas_call x0 -> x1, Pallas kernels: none -> 78.5 us  [per_device(): pl.pallas_call(kernel, out_shape=(jax.ShapeDtypeStruct((1, FFD, D), BF16)...]
    gather x4 -> x0, local copies, waits for them, and re-layouts: 36.3 us -> none  [the longest x2 22.2 us: per_device(): grad_out[tokens_of] * slot_live[:, None]]
    all_to_all x3 -> x0, starting transfers between devices: 33.4 us -> none  [the longest x1 15.4 us: per_device(): lax.all_to_all(gate_slots, ('dp', 'edp'), split_axis=0, concat_axis=0, ti...]
    another operation x3 -> x0, other arithmetic: 18.2 us -> none
    dot_general x2 -> x0, matrix products: 16 us -> none  [the longest x1 8.46 us: dense_products(): weight_grad = jnp.dot(scaled, row_block, preferred_element_type=jnp.float32)]
    reshape x4 -> x0, local copies, waits for them, and re-layouts: 14.3 us -> none  [the longest x1 14 us: per_device(): row_block = arrived.reshape(slot_total, model_width)]
  transfers between devices with their start and end apart: 3 -> 0, of which waited for: 2 -> 0; matrix products, arithmetic and copies ran while one was open for 5% -> 0% of each run, Pallas kernels for 0% -> 0%
where the time goes in v2:
time: 81.9 us; the launch traced here: 81.8 us
  Pallas kernels  78.5 us (96%)
  other arithmetic  2.01 us (2%)
    pallas_call x1, Pallas kernels, per_device(): pl.pallas_call(kernel, out_shape=(jax.ShapeDtypeStruct((1, FFD, D), BF16)...  78.5 us
    convert_element_type x1, other arithmetic, per_device(): down_grad = (part.astype(F32) * factor[0, 0]).astype(BF16)  2.01 us

profile of v2, /device:TPU:1, one launch (start us, length us, event | category | flops | bytes accessed | tf_op | source)
XLA Modules:
  0.0 81.8 jit_solution(11597622097992786124)
XLA Ops:
  0.6 78.5 %moe_down_backward.1 = (bf16[1,192,4096]{2,1,0:T(8,128)(2,1)S(1)}, f32[1,1]{1,0:T(1,128)}, f32[8,128]{1,0:T(8,128)S(1)}) custom-call(s32[8,128]{1,0:T(8,128)} %bitcast.5, bf16[8,128]{1,0:T(8,128)(2,1)} %bitcast.6, bf16[128,4096]{1,0:T(8,128)(2,1)} %grad_hbm.1, bf16[1,192,1280]{2,1,0:T(8,128)(2,1)} %hid_hbm.1, bf16[1,192,4096]{2,1,0:T(8,128)(2,1)} %w_hbm.1), custom_call_target="tpu_custom_call" | custom-call | flops 4026531840 | bytes 8388608 | tf_op jit(solution)/shard_map/moe_down_backward/pallas_call | solution.py:566
  79.2 2.0 %multiply_convert_fusion = bf16[1,192,4096]{2,1,0:T(8,128)(2,1)} fusion(bf16[1,192,4096]{2,1,0:T(8,128)(2,1)S(1)} %get-tuple-element.5, f32[]{:T(128)} %bitcast.2), kind=kLoop, calls=%fused_computation | loop fusion | flops 2359296 | bytes 3145732 | tf_op jit(solution)/shard_map/convert_element_type | solution.py:624
  81.2 0.6 copy.8

commit v3 on v2

--- a/solution.py
+++ b/solution.py
@@ -24,10 +24,18 @@
     rest = lambda parts: [(r, whole, CAP) for r in parts if CAP > whole]
     head = lambda parts: [(r, 0, whole) for r in parts]
     if ZS == 8:
-        return [head([0, 1, 2]), head([3, 4]) + rest([0, 1, 2, 3]), head([5, 6]), head([7]) + rest([4, 5, 6, 7])]
+        return [
+            head([0]), head([1, 2]), head([3, 4]) + rest([0, 1, 2, 3]), head([5, 6]), head([7]) + rest([4, 5, 6, 7])]
     if ZS == 4:
-        return [head([0, 1, 2]), head([3]) + rest([0, 1, 2, 3])]
-    return [head([0, 1]) + rest([0, 1])]
+        return [head([0]), head([1, 2]), head([3]) + rest([0, 1, 2, 3])]
+    return [head([0]), head([1]) + rest([0, 1])]
+
+
+def messages(q):
+    count = len(slot_groups())
+    if q == 0:
+        return [(g, g) for g in range(count)]
+    return [(0, 1), (2, 2), (3, 4)] if count == 5 else [(0, 1), (2, 2)] if count == 3 else [(0, 1)]
 
 
 K_Q, K_GY, K_RY, K_RZ, K_GG = range(5)
@@ -236,8 +244,9 @@
     for p in pieces[NR // 2:]:
         get_t[p].wait()
     ring(1, pieces[NR // 2:])
-    for i in near_x:
-        send_w(0, i).start()
+    for q in range(NQ):
+        for i in near_x:
+            send_w(q, i).start()
 
     def got_h(i):
         dev, there = peers_x[i]
@@ -254,10 +263,8 @@
             for i in range(2):
                 got_h(2 - i)
                 pass_h(i).start()
-            send_w(0, 0).start()
-        for q in range(1, NQ):
-            for i in range(XS - 1):
-                send_w(q, i).start()
+            for q in range(NQ):
+                send_w(q, 0).start()
 
     heard = set()
 
@@ -283,19 +290,23 @@
                 sel[g][e * n:(e + 1) * n, (r - lo) * TOK:(r - lo + 1) * TOK] = (
                     want == tile[e:e + 1, :]).astype(F32).astype(BF16)
 
-    def part_of(expert, g):
-        return pl.ds(pl.multiple_of(expert * BLK + firsts[g], 16), sizes[g])
-
-    def send_y(q, g, i):
+    def span_of(m):
+        return firsts[m[0]], firsts[m[1]] + sizes[m[1]]
+
+    def part_of(expert, m):
+        lo, hi = span_of(m)
+        return pl.ds(pl.multiple_of(expert * BLK + lo, 16), hi - lo)
+
+    def send_y(q, m, i):
         dev, there = out_y[i]
+        lo, hi = span_of(m)
         return remote(
-            sendb.at[q, there, firsts[g]:firsts[g] + sizes[g]], rows.at[q, part_of(me8, g)],
-            ys.at[q, g, i], yr.at[q, g, me8], dev)
-
-    def own_rows(q, g):
+            sendb.at[q, there, lo:hi], rows.at[q, part_of(me8, m)], ys.at[q, m[1], i], yr.at[q, m[1], me8], dev)
+
+    def own_rows(q, m):
+        lo, hi = span_of(m)
         return pltpu.make_async_copy(
-            sendb.at[q, me8, firsts[g]:firsts[g] + sizes[g]], rows.at[q, part_of(me8, g)],
-            loc.at[1 + NR + NQ + q * GROUPS + g])
+            sendb.at[q, me8, lo:hi], rows.at[q, part_of(me8, m)], loc.at[1 + NR + NQ + q * GROUPS + m[1]])
 
     def select(q, g):
         if g >= GROUPS:
@@ -309,9 +320,11 @@
             at = (p - q * NR // NQ) * DR
             for e in range(E8):
                 sendb[q, e, firsts[g]:firsts[g] + n, at:at + DR] = got[e * n:(e + 1) * n]
-        for i in range(E8 - 1):
-            send_y(q, g, i).start()
-        own_rows(q, g).start()
+        for m in messages(q):
+            if m[1] == g:
+                for i in range(E8 - 1):
+                    send_y(q, m, i).start()
+                own_rows(q, m).start()
 
     def gy_copy(i):
         dev, there = out_y[i]
@@ -330,26 +343,29 @@
             gy_copy(i).start()
 
     first, second = pieces[:NR // 2], pieces[NR // 2:]
-    ring(2, first)
     build_sel(0)
     select(0, 0)
-    ring(2, second)
     select(1, 0)
-    ring(3, first)
+    ring(2, first)
     build_sel(1)
     select(0, 1)
+    ring(2, second)
+    select(1, 1)
+    ring(3, first)
+    build_sel(2)
+    select(0, 2)
     ring(3, second)
-    select(1, 1)
-    build_sel(2)
+    select(1, 2)
     gates_on()
+    build_sel(3)
     ring(4, first)
-    select(0, 2)
+    select(0, 3)
     more_x()
-    build_sel(3)
+    build_sel(4)
     ring(4, second)
-    select(1, 2)
-    select(0, 3)
     select(1, 3)
+    select(0, 4)
+    select(1, 4)
 
     if XS == 4:
         for i in range(2):
@@ -381,12 +397,13 @@
                 ws.at[q, 0], wr.at[q, there], dev).wait_recv()
 
     def wait_rows(q):
-        for g in range(GROUPS):
-            own_rows(q, g).wait()
+        for m in messages(q):
+            own_rows(q, m).wait()
+            lo, hi = span_of(m)
             for dev, there in out_y:
                 remote(
-                    sendb.at[q, there, firsts[g]:firsts[g] + sizes[g]], rows.at[q, part_of(there, g)],
-                    ys.at[q, g, 0], yr.at[q, g, there], dev).wait_recv()
+                    sendb.at[q, there, lo:hi], rows.at[q, part_of(there, m)],
+                    ys.at[q, m[1], 0], yr.at[q, m[1], there], dev).wait_recv()
 
     def send_o(q, i):
         dev, there = peers_x[i]
@@ -440,6 +457,7 @@
     lax.fori_loop(0, SLOTS // PB, fold_first, 0)
     for q in range(1, NQ):
         squares = products(q, squares)
+    for q in range(1, NQ):
         turned(q)
 
     def fold_last(j, carry):
@@ -479,9 +497,9 @@
     for q in range(NQ):
         for i in range(XS - 1):
             send_w(q, i).wait_send()
-        for g in range(GROUPS):
+        for m in messages(q):
             for i in range(E8 - 1):
-                send_y(q, g, i).wait_send()
+                send_y(q, m, i).wait_send()
     for i in near_x:
         send_h(i).wait_send()
     if XS == 4:

time: 81.9 us -> 78.1 us (0.954)
  Pallas kernels: 78.5 us -> 74.6 us
    pallas_call x1, Pallas kernels: 78.5 us -> 74.6 us  [per_device(): pl.pallas_call(kernel, out_shape=(jax.ShapeDtypeStruct((1, FFD, D), BF16)...]
where the time goes in v3:
time: 78.1 us; the launch traced here: 77.8 us
  Pallas kernels  74.6 us (96%)
  other arithmetic  2.01 us (3%)
    pallas_call x1, Pallas kernels, per_device(): pl.pallas_call(kernel, out_shape=(jax.ShapeDtypeStruct((1, FFD, D), BF16)...  74.6 us
    convert_element_type x1, other arithmetic, per_device(): down_grad = (part.astype(F32) * factor[0, 0]).astype(BF16)  2.01 us

profile of v3, /device:TPU:1, one launch (start us, length us, event | category | flops | bytes accessed | tf_op | source)
XLA Modules:
  0.0 77.8 jit_solution(4315998667005654499)
XLA Ops:
  0.6 74.6 %moe_down_backward.1 = (bf16[1,192,4096]{2,1,0:T(8,128)(2,1)S(1)}, f32[1,1]{1,0:T(1,128)}, f32[8,128]{1,0:T(8,128)S(1)}) custom-call(s32[8,128]{1,0:T(8,128)} %bitcast.5, bf16[8,128]{1,0:T(8,128)(2,1)} %bitcast.6, bf16[128,4096]{1,0:T(8,128)(2,1)} %grad_hbm.1, bf16[1,192,1280]{2,1,0:T(8,128)(2,1)} %hid_hbm.1, bf16[1,192,4096]{2,1,0:T(8,128)(2,1)} %w_hbm.1), custom_call_target="tpu_custom_call" | custom-call | flops 4026531840 | bytes 8388608 | tf_op jit(solution)/shard_map/moe_down_backward/pallas_call | solution.py:584
  75.2 2.0 %multiply_convert_fusion = bf16[1,192,4096]{2,1,0:T(8,128)(2,1)} fusion(bf16[1,192,4096]{2,1,0:T(8,128)(2,1)S(1)} %get-tuple-element.5, f32[]{:T(128)} %bitcast.2), kind=kLoop, calls=%fused_computation | loop fusion | flops 2359296 | bytes 3145732 | tf_op jit(solution)/shard_map/convert_element_type | solution.py:642
  77.2 0.6 copy.8

commit v4 on v3

--- a/solution.py
+++ b/solution.py
@@ -35,7 +35,7 @@
     count = len(slot_groups())
     if q == 0:
         return [(g, g) for g in range(count)]
-    return [(0, 1), (2, 2), (3, 4)] if count == 5 else [(0, 1), (2, 2)] if count == 3 else [(0, 1)]
+    return [(0, 0), (1, 1), (2, 2), (3, 4)] if count == 5 else [(0, 1), (2, 2)] if count == 3 else [(0, 1)]
 
 
 K_Q, K_GY, K_RY, K_RZ, K_GG = range(5)
@@ -49,7 +49,7 @@
     routes_hbm, gates_hbm, grad_hbm, hid_hbm, w_hbm,
     out_hbm, factor_ref, gg_ref,
     routes_ref, gates_ref, tok, sel, sendb, rows, qsend, qrecv, gsy, gtab,
-    hraw, perm, hx, hs, hxt, wv, wgs, gbk, acc, bp, spread_t, rsend, ry, rzs, rz, gg,
+    hraw, perm, hx, hs, hxt, wv, wgs, gbk, acc, spread_t, rsend, ry, rzs, rz, gg,
     loc, zs, zr, ys, yr, ws, wr, hsn, hr, hfs, hfr, osn, orc, sms, smr,
 ):
     E8 = CS * YS
@@ -245,7 +245,7 @@
         get_t[p].wait()
     ring(1, pieces[NR // 2:])
     for q in range(NQ):
-        for i in near_x:
+        for i in near_x + [i for i in range(XS - 1) if i not in near_x]:
             send_w(q, i).start()
 
     def got_h(i):
@@ -258,13 +258,11 @@
         part = hx.at[pl.ds(pl.multiple_of(frm * FFD + i * (FFD // 2), FFD // 2), FFD // 2)]
         return remote(part, part, hfs.at[i], hfr.at[i], peers_x[2 if i == 1 else 1][0])
 
-    def more_x():
+    def far_h():
         if XS == 4:
             for i in range(2):
                 got_h(2 - i)
                 pass_h(i).start()
-            for q in range(NQ):
-                send_w(q, 0).start()
 
     heard = set()
 
@@ -360,22 +358,45 @@
     build_sel(3)
     ring(4, first)
     select(0, 3)
-    more_x()
     build_sel(4)
     ring(4, second)
     select(1, 3)
     select(0, 4)
     select(1, 4)
-
-    if XS == 4:
-        for i in range(2):
-            part = hx.at[pl.ds(pl.multiple_of(peers_x[0][1] * FFD + i * (FFD // 2), FFD // 2), FFD // 2)]
-            remote(part, part, hfs.at[i], hfr.at[i], peers_x[1][0]).wait_recv()
-    else:
-        for i in near_x:
+    far_h()
+
+    def turn(there):
+        for j in range(SLOTS // PB):
+            hxt[there, j * PB:(j + 1) * PB, :] = hx[blk(there, FFD), j * PB:(j + 1) * PB].T
+
+    def wait_w(q, i):
+        dev, there = peers_x[i]
+        remote(
+            w_hbm.at[0, :, col(x * DX + q * DQ, DQ)], wv.at[q, blk(there, FFD)],
+            ws.at[q, 0], wr.at[q, there], dev).wait_recv()
+
+    def turned(q, there):
+        return jnp.dot(hxt[there], wv[q, blk(there, FFD), :], preferred_element_type=F32)
+
+    turn(x)
+    for q in range(NQ):
+        own_w(q).wait()
+        gbk[q] = turned(q, x)
+    for i in near_x:
+        if XS < 4:
             got_h(i)
-    for j in range(SLOTS // PB):
-        hxt[j * PB:(j + 1) * PB, :] = hx[:, j * PB:(j + 1) * PB].T
+        turn(peers_x[i][1])
+        for q in range(NQ):
+            wait_w(q, i)
+            gbk[q] = gbk[q] + turned(q, peers_x[i][1])
+    for copy in sent:
+        copy.wait_send()
+    for i in range(ZS - 1):
+        q_copy(i).wait_send()
+    for i in near_x:
+        send_h(i).wait_send()
+        for q in range(NQ):
+            send_w(q, i).wait_send()
     for dev, there in out_y:
         remote(gsy.at[there], gtab.at[there], sms.at[K_GY, 0], smr.at[K_GY, there], dev).wait_recv()
     spread = (iota((TOK, SLOTS), 0) == place).astype(F32)
@@ -385,16 +406,22 @@
     gate_all = jnp.dot(gtab[...].reshape(EXP, TOK).astype(BF16), spread, preferred_element_type=F32)
     pick = iota((EXP, SLOTS), 0) == source
     gate_lane = jnp.sum(jnp.where(pick, gate_all, 0.0), axis=0, keepdims=True)
-    for i in range(XS):
-        part = slice(i * FFD, (i + 1) * FFD)
+
+    def gated(there):
+        part = blk(there, FFD)
         hs[part, :] = (hx[part, :].astype(F32) * gate_lane).astype(BF16)
 
-    def wait_w(q):
-        own_w(q).wait()
-        for dev, there in peers_x:
-            remote(
-                w_hbm.at[0, :, col(x * DX + q * DQ, DQ)], wv.at[q, blk(there, FFD)],
-                ws.at[q, 0], wr.at[q, there], dev).wait_recv()
+    gated(x)
+    for i in near_x:
+        gated(peers_x[i][1])
+
+    def get_far():
+        for i in range(2):
+            part = hx.at[pl.ds(pl.multiple_of(peers_x[0][1] * FFD + i * (FFD // 2), FFD // 2), FFD // 2)]
+            remote(part, part, hfs.at[i], hfr.at[i], peers_x[1][0]).wait_recv()
+        turn(peers_x[0][1])
+        gated(peers_x[0][1])
+
 
     def wait_rows(q):
         for m in messages(q):
@@ -418,8 +445,10 @@
 
     def products(q, squares):
         wait_rows(q)
-        for i in range(XS):
+        for i in near_x + [XS - 1] + [i for i in range(XS - 1) if i not in near_x]:
             there = x if i == XS - 1 else peers_x[i][1]
+            if i not in near_x and i < XS - 1 and q == 0:
+                get_far()
             wg = jnp.dot(hs[blk(there, FFD), :], rows[q], preferred_element_type=F32)
             wgs[q, blk(there, FFD), :] = wg.astype(BF16)
             if i == XS - 1:
@@ -429,54 +458,37 @@
             squares = squares + jnp.sum((wg * wg).reshape(FFD // 8, 8, DQ), axis=0)
         return squares
 
-    def turned(q):
-        wait_w(q)
-
-        def body(j, carry):
-            at = pl.ds(pl.multiple_of(j * PB, PB), PB)
-            gbk[q, at, :] = jnp.dot(hxt[at, :], wv[q], preferred_element_type=F32)
-            return carry
-
-        lax.fori_loop(0, SLOTS // PB, body, 0)
-
-    def fold(q, at):
-        both = gbk[q, at, :] * rows[q, at, :].astype(F32)
+    def fold(q):
+        got = gbk[q]
+        if XS == 4:
+            wait_w(q, 0)
+            got = got + turned(q, peers_x[0][1])
+        both = got * rows[q].astype(F32)
         total = both[:, 0:128]
         for i in range(1, DQ // 128):
             total = total + both[:, i * 128:(i + 1) * 128]
         return total
 
-    turned(0)
     squares = products(0, jnp.zeros((8, DQ), F32))
-
-    def fold_first(j, carry):
-        at = pl.ds(pl.multiple_of(j * PB, PB), PB)
-        acc[at, :] = fold(0, at)
-        return carry
-
-    lax.fori_loop(0, SLOTS // PB, fold_first, 0)
+    acc[...] = fold(0)
+    for i in range(E8 - 1):
+        gy_copy(i).wait_send()
+        for m in messages(0):
+            send_y(0, m, i).wait_send()
     for q in range(1, NQ):
         squares = products(q, squares)
     for q in range(1, NQ):
-        turned(q)
-
-    def fold_last(j, carry):
-        at = pl.ds(pl.multiple_of(j * PB, PB), PB)
-        total = acc[at, :]
-        for q in range(1, NQ):
-            total = total + fold(q, at)
-        bp[at, :] = spread_t[at, :] * jnp.sum(total, axis=1, keepdims=True)
-        return carry
-
-    lax.fori_loop(0, SLOTS // PB, fold_last, 0)
-    tile = squares[:, 0:128]
-    for i in range(1, DQ // 128):
-        tile = tile + squares[:, i * 128:(i + 1) * 128]
-
-    back = jnp.dot(pick.astype(F32), bp[...], preferred_element_type=F32, precision=lax.Precision.HIGHEST)
+        acc[...] += fold(q)
+    by_place = spread_t[...] * jnp.sum(acc[...], axis=1, keepdims=True)
+    own_square = jnp.sum(jnp.sum(squares, axis=1, keepdims=True), axis=0, keepdims=True)
+
+    high = by_place.astype(BF16)
+    low = (by_place - high.astype(F32)).astype(BF16)
+    pick_b = pick.astype(F32).astype(BF16)
+    back = jnp.dot(pick_b, high, preferred_element_type=F32) + jnp.dot(pick_b, low, preferred_element_type=F32)
+    back = jnp.where(iota((EXP, TOK), 1) == TOK - 1, own_square, back)
     for e in range(E8):
-        rsend[e, 0:ZS] = back[e * ZS:(e + 1) * ZS]
-        rsend[e, ZS:ZS + 8] = tile
+        rsend[e] = back[e * ZS:(e + 1) * ZS]
 
     def ry_copy(i):
         dev, there = all_y[i]
@@ -494,40 +506,30 @@
         ry_copy(i).start()
     ry[h * E8 + me8] = rsend[me8]
 
-    for q in range(NQ):
-        for i in range(XS - 1):
-            send_w(q, i).wait_send()
+    for q in range(1, NQ):
         for m in messages(q):
             for i in range(E8 - 1):
                 send_y(q, m, i).wait_send()
-    for i in near_x:
-        send_h(i).wait_send()
     if XS == 4:
+        for q in range(NQ):
+            send_w(q, 0).wait_send()
         for i in range(2):
             pass_h(i).wait_send()
-    for copy in sent:
-        copy.wait_send()
-    for i in range(ZS - 1):
-        q_copy(i).wait_send()
-    for i in range(E8 - 1):
-        gy_copy(i).wait_send()
 
     for dev, there in all_y:
         there = lax.rem(dev[0], HS) * E8 + there
         remote(rsend.at[0], ry.at[there], sms.at[K_RY, 0], smr.at[K_RY, there], dev).wait_recv()
 
-    tile = jnp.sum(ry[:, ZS:ZS + 8, :], axis=0)
     for r in range(ZS):
         for e in range(E8):
             rzs[r, e:e + 1, :] = ry[e, r:r + 1, :] + ry[E8 + e, r:r + 1, :]
-        rzs[r, E8:E8 + 8] = tile
     for i in range(ZS - 1):
         rz_copy(i).start()
     rz[z] = rzs[0]
     for dev, there in peers_z:
         remote(rzs.at[0], rz.at[there], sms.at[K_RZ, 0], smr.at[K_RZ, there], dev).wait_recv()
 
-    by_expert = rz[:, 0:E8, :].reshape(EXP, TOK)
+    by_expert = rz[...].reshape(EXP, TOK)
     qt2 = qsend[:, 0:E8, :].reshape(EXP, TOK)
     value = jnp.zeros((EXP, TOK), F32)
     for p in range(CAP):
@@ -535,14 +537,14 @@
     for k in range(TOP):
         gg[x, k:k + 1, :] = jnp.sum(
             jnp.where(routes_ref[k:k + 1, :] == eidx, value, 0.0), axis=0, keepdims=True)
-    gg[x, 8:16, :] = jnp.sum(rz[:, E8:E8 + 8, :], axis=0)
+    gg[x, 8:16, :] = jnp.broadcast_to(
+        jnp.sum(by_expert[:, TOK - 1:TOK], axis=0, keepdims=True), (8, TOK))
     for i in range(XS - 1):
         gg_copy(i).start()
     for dev, there in peers_x:
         remote(gg.at[x], gg.at[there], sms.at[K_GG, 0], smr.at[K_GG, there], dev).wait_recv()
 
-    total = jnp.sum(gg[:, 8:16, :], axis=0)
-    total = jnp.sum(jnp.sum(total, axis=1, keepdims=True), axis=0, keepdims=True)
+    total = jnp.sum(gg[:, 8:16, :], axis=0)[0:1, 0:1]
     limit = clip_ratio * math.sqrt(FFD * D * TPS * EXP)
     factor = jnp.minimum(1.0, limit / (jnp.sqrt(total) + 1e-06))
     factor_ref[...] = factor
@@ -605,17 +607,16 @@
             vm((SLOTS, SLOTS), BF16),
             vm((XS * FFD, SLOTS), BF16),
             vm((XS * FFD, SLOTS), BF16),
-            vm((SLOTS, XS * FFD), BF16),
+            vm((XS, SLOTS, FFD), BF16),
             vm((NQ, XS * FFD, DQ), BF16),
             vm((NQ, XS * FFD, DQ), BF16),
             vm((NQ, SLOTS, DQ), F32),
             vm((SLOTS, 128), F32),
             vm((SLOTS, TOK), F32),
-            vm((SLOTS, TOK), F32),
-            vm((E8, ZS + 8, TOK), F32),
-            vm((HS * E8, ZS + 8, TOK), F32),
-            vm((ZS, E8 + 8, TOK), F32),
-            vm((ZS, E8 + 8, TOK), F32),
+            vm((E8, ZS, TOK), F32),
+            vm((HS * E8, ZS, TOK), F32),
+            vm((ZS, E8, TOK), F32),
+            vm((ZS, E8, TOK), F32),
             vm((XS, 16, TOK), F32),
             dma((3 + NR + 2 * NQ + NQ * GROUPS,)),
             dma((NR, ZS)),

time: 78.1 us -> 74.5 us (0.954)
  Pallas kernels: 74.6 us -> 71.1 us
    pallas_call x1, Pallas kernels: 74.6 us -> 71.1 us  [per_device(): pl.pallas_call(kernel, out_shape=(jax.ShapeDtypeStruct((1, FFD, D), BF16)...]
where the time goes in v4:
time: 74.5 us; the launch traced here: 74.4 us
  Pallas kernels  71.1 us (95%)
  other arithmetic  2.01 us (3%)
    pallas_call x1, Pallas kernels, per_device(): pl.pallas_call(kernel, out_shape=(jax.ShapeDtypeStruct((1, FFD, D), BF16)...  71.1 us
    convert_element_type x1, other arithmetic, per_device(): down_grad = (part.astype(F32) * factor[0, 0]).astype(BF16)  2.01 us

profile of v4, /device:TPU:1, one launch (start us, length us, event | category | flops | bytes accessed | tf_op | source)
XLA Modules:
  0.0 74.4 jit_solution(9141076319302788053)
XLA Ops:
  0.6 71.1 %moe_down_backward.1 = (bf16[1,192,4096]{2,1,0:T(8,128)(2,1)S(1)}, f32[1,1]{1,0:T(1,128)}, f32[8,128]{1,0:T(8,128)S(1)}) custom-call(s32[8,128]{1,0:T(8,128)} %bitcast.5, bf16[8,128]{1,0:T(8,128)(2,1)} %bitcast.6, bf16[128,4096]{1,0:T(8,128)(2,1)} %grad_hbm.1, bf16[1,192,1280]{2,1,0:T(8,128)(2,1)} %hid_hbm.1, bf16[1,192,4096]{2,1,0:T(8,128)(2,1)} %w_hbm.1), custom_call_target="tpu_custom_call" | custom-call | flops 4026531840 | bytes 8388608 | tf_op jit(solution)/shard_map/moe_down_backward/pallas_call | solution.py:586
  71.7 2.0 %multiply_convert_fusion = bf16[1,192,4096]{2,1,0:T(8,128)(2,1)} fusion(bf16[1,192,4096]{2,1,0:T(8,128)(2,1)S(1)} %get-tuple-element.5, f32[]{:T(128)} %bitcast.2), kind=kLoop, calls=%fused_computation | loop fusion | flops 2359296 | bytes 3145732 | tf_op jit(solution)/shard_map/convert_element_type | solution.py:643
  73.8 0.6 copy.8

commit v5 on v4

--- a/solution.py
+++ b/solution.py
@@ -541,15 +541,6 @@
         jnp.sum(by_expert[:, TOK - 1:TOK], axis=0, keepdims=True), (8, TOK))
     for i in range(XS - 1):
         gg_copy(i).start()
-    for dev, there in peers_x:
-        remote(gg.at[x], gg.at[there], sms.at[K_GG, 0], smr.at[K_GG, there], dev).wait_recv()
-
-    total = jnp.sum(gg[:, 8:16, :], axis=0)[0:1, 0:1]
-    limit = clip_ratio * math.sqrt(FFD * D * TPS * EXP)
-    factor = jnp.minimum(1.0, limit / (jnp.sqrt(total) + 1e-06))
-    factor_ref[...] = factor
-    gg_ref[...] = jnp.sum(gg[:, 0:TOP, :], axis=0)
-
     for q in range(NQ):
         own_o(q).wait()
         for i in range(XS - 1):
@@ -562,8 +553,33 @@
         rz_copy(i).wait_send()
     for i in range(len(all_y)):
         ry_copy(i).wait_send()
+
+    for dev, there in peers_x:
+        remote(gg.at[x], gg.at[there], sms.at[K_GG, 0], smr.at[K_GG, there], dev).wait_recv()
+
+    total = jnp.sum(gg[:, 8:16, :], axis=0)[0:1, 0:1]
+    limit = clip_ratio * math.sqrt(FFD * D * TPS * EXP)
+    factor = jnp.minimum(1.0, limit / (jnp.sqrt(total) + 1e-06))
+    factor_ref[...] = jnp.broadcast_to(factor, factor_ref.shape)
+    gg_ref[...] = jnp.sum(gg[:, 0:TOP, :], axis=0)
     for i in range(XS - 1):
         gg_copy(i).wait_send()
+
+
+def scale_kernel(part_ref, factor_ref, gg_in, out_hbm, gg_out, buf, done, gg_done):
+    gg_copy = pltpu.make_async_copy(gg_in, gg_out, gg_done)
+    gg_copy.start()
+    factor = factor_ref[0:1, 0:1]
+    high = buf.shape[1]
+    copies = []
+    for i in range(buf.shape[0]):
+        at = slice(i * high, (i + 1) * high)
+        buf[i] = (part_ref[0, at, :].astype(F32) * factor).astype(BF16)
+        copies.append(pltpu.make_async_copy(buf.at[i], out_hbm.at[0, at, :], done.at[i]))
+        copies[-1].start()
+    gg_copy.wait()
+    for copy in copies:
+        copy.wait()
 
 
 def per_device(grad_out, routes, gates, hidden, w_down):
@@ -587,7 +603,7 @@
         kernel,
         out_shape=(
             jax.ShapeDtypeStruct((1, FFD, D), BF16),
-            jax.ShapeDtypeStruct((1, 1), F32),
+            jax.ShapeDtypeStruct((8, 128), F32),
             jax.ShapeDtypeStruct((TOP, TOK), F32),
         ),
         in_specs=[in_hbm] * 5,
@@ -640,7 +656,20 @@
             flops=2 * 2 * SLOTS * FFD * D, bytes_accessed=8 * 1024 * 1024, transcendentals=0),
         name="moe_down_backward",
     )(*[pltpu.with_memory_space_constraint(a, pltpu.HBM) for a in (routes.T, gates.T, grad_out, hidden, w_down)])
-    down_grad = (part.astype(F32) * factor[0, 0]).astype(BF16)
+    high = 32 if FFD % 32 == 0 else FFD
+    down_grad, gate_grad = pl.pallas_call(
+        scale_kernel,
+        out_shape=(
+            jax.ShapeDtypeStruct((1, FFD, D), BF16),
+            jax.ShapeDtypeStruct((TOP, TOK), F32),
+        ),
+        in_specs=[in_vmem, in_vmem, in_vmem],
+        out_specs=(any_space, any_space),
+        scratch_shapes=[vm((FFD // high, high, D), BF16), dma((FFD // high,)), dma(())],
+        compiler_params=pltpu.CompilerParams(vmem_limit_bytes=8 * 1024 * 1024),
+        cost_estimate=pl.CostEstimate(flops=FFD * D, bytes_accessed=4 * FFD * D, transcendentals=0),
+        name="scale_products",
+    )(part, factor, gate_grad)
     return (down_grad, gate_grad.T)
 
 

time: 74.5 us -> 72.7 us (0.976)
  other arithmetic: 2.01 us -> 0 us
  Pallas kernels: 71.1 us -> 71.9 us
    convert_element_type x1 -> x0, other arithmetic: 2.01 us -> none  [per_device(): down_grad = (part.astype(F32) * factor[0, 0]).astype(BF16)]
    pallas_call x0 -> x1, Pallas kernels: none -> 1.29 us  [per_device(): pl.pallas_call(scale_kernel, out_shape=(jax.ShapeDtypeStruct((1, FFD, D),...]
where the time goes in v5:
time: 72.7 us; the launch traced here: 72.5 us
  Pallas kernels  71.9 us (99%)
    pallas_call x1, Pallas kernels, per_device(): pl.pallas_call(kernel, out_shape=(jax.ShapeDtypeStruct((1, FFD, D), BF16)...  70.6 us

profile of v5, /device:TPU:1, one launch (start us, length us, event | category | flops | bytes accessed | tf_op | source)
XLA Modules:
  0.0 72.5 jit_solution(5212194851837231858)
XLA Ops:
  0.6 70.6 %moe_down_backward.1 = (bf16[1,192,4096]{2,1,0:T(8,128)(2,1)S(1)}, f32[8,128]{1,0:T(8,128)S(1)}, f32[8,128]{1,0:T(8,128)S(1)}) custom-call(s32[8,128]{1,0:T(8,128)} %bitcast.3, bf16[8,128]{1,0:T(8,128)(2,1)} %bitcast.5, bf16[128,4096]{1,0:T(8,128)(2,1)} %grad_hbm.1, bf16[1,192,1280]{2,1,0:T(8,128)(2,1)} %hid_hbm.1, bf16[1,192,4096]{2,1,0:T(8,128)(2,1)} %w_hbm.1), custom_call_target="tpu_custom_call" | custom-call | flops 4026531840 | bytes 8388608 | tf_op jit(solution)/shard_map/moe_down_backward/pallas_call | solution.py:602
  71.2 1.3 %scale_products.1 = (bf16[1,192,4096]{2,1,0:T(8,128)(2,1)}, f32[8,128]{1,0:T(8,128)}) custom-call(bf16[1,192,4096]{2,1,0:T(8,128)(2,1)S(1)} %get-tuple-element.7.part_ref, f32[8,128]{1,0:T(8,128)S(1)} %get-tuple-element.8.factor_ref, f32[8,128]{1,0:T(8,128)S(1)} %get-tuple-element.9.gg_in), custom_call_target="tpu_custom_call" | custom-call | flops 786432 | bytes 3145728 | tf_op jit(solution)/shard_map/scale_products/pallas_call | solution.py:660

commit v6 on v5

--- a/solution.py
+++ b/solution.py
@@ -46,9 +46,9 @@
 
 
 def kernel(
-    routes_hbm, gates_hbm, grad_hbm, hid_hbm, w_hbm,
+    routes_hbm, gates_ref, grad_hbm, hid_hbm, w_hbm,
     out_hbm, factor_ref, gg_ref,
-    routes_ref, gates_ref, tok, sel, sendb, rows, qsend, qrecv, gsy, gtab,
+    routes_ref, tok, sel, sendb, rows, qsend, qrecv, gsy, gtab,
     hraw, perm, hx, hs, hxt, wv, wgs, gbk, acc, spread_t, rsend, ry, rzs, rz, gg,
     loc, zs, zr, ys, yr, ws, wr, hsn, hr, hfs, hfr, osn, orc, sms, smr,
 ):
@@ -115,8 +115,6 @@
 
     get_r = pltpu.make_async_copy(routes_hbm, routes_ref, loc.at[1 + NR + 2 * NQ + NQ * GROUPS])
     get_r.start()
-    get_g = pltpu.make_async_copy(gates_hbm, gates_ref, loc.at[2 + NR + 2 * NQ + NQ * GROUPS])
-    get_g.start()
     get_t = [
         pltpu.make_async_copy(grad_hbm.at[:, col(x * DX + p * DR, DR)], tok.at[p, 0:TOK], loc.at[1 + p])
         for p in range(NR)
@@ -134,13 +132,13 @@
         own_w(q).start()
 
     get_r.wait()
-    get_g.wait()
+    routes_v = routes_ref[...]
     eidx = iota((EXP, TOK), 0)
     chosen = jnp.zeros((EXP, TOK), F32)
     gate_t = jnp.zeros((EXP, TOK), F32)
     gates_f = gates_ref[...].astype(F32)
     for k in range(TOP):
-        hit = routes_ref[k:k + 1, :] == eidx
+        hit = routes_v[k:k + 1, :] == eidx
         chosen = jnp.where(hit, 1.0, chosen)
         gate_t = jnp.where(hit, gates_f[k:k + 1, :], gate_t)
     earlier = (iota((TOK, TOK), 0) < iota((TOK, TOK), 1)).astype(F32).astype(BF16)
@@ -333,9 +331,9 @@
             if r not in heard:
                 heard.add(r)
                 remote(qsend.at[0], qrecv.at[r], sms.at[K_Q, 0], smr.at[K_Q, r], peers_z[0][0]).wait_recv()
-        for r in range(ZS):
-            for e in range(E8):
-                gsy[e, r:r + 1, :] = qrecv[r, E8 + e:E8 + e + 1, :]
+        by_source = [qrecv[r, E8:2 * E8] for r in range(ZS)]
+        for e in range(E8):
+            gsy[e] = jnp.concatenate([tile[e:e + 1] for tile in by_source], axis=0)
         gtab[me8] = gsy[me8]
         for i in range(E8 - 1):
             gy_copy(i).start()
@@ -367,7 +365,7 @@
 
     def turn(there):
         for j in range(SLOTS // PB):
-            hxt[there, j * PB:(j + 1) * PB, :] = hx[blk(there, FFD), j * PB:(j + 1) * PB].T
+            hxt[there, j * PB:(j + 1) * PB, 0:FFD] = hx[blk(there, FFD), j * PB:(j + 1) * PB].T
 
     def wait_w(q, i):
         dev, there = peers_x[i]
@@ -376,7 +374,7 @@
             ws.at[q, 0], wr.at[q, there], dev).wait_recv()
 
     def turned(q, there):
-        return jnp.dot(hxt[there], wv[q, blk(there, FFD), :], preferred_element_type=F32)
+        return jnp.dot(hxt[there, :, 0:FFD], wv[q, blk(there, FFD), :], preferred_element_type=F32)
 
     turn(x)
     for q in range(NQ):
@@ -520,9 +518,9 @@
         there = lax.rem(dev[0], HS) * E8 + there
         remote(rsend.at[0], ry.at[there], sms.at[K_RY, 0], smr.at[K_RY, there], dev).wait_recv()
 
+    by_sender = [ry[e] + ry[E8 + e] for e in range(E8)]
     for r in range(ZS):
-        for e in range(E8):
-            rzs[r, e:e + 1, :] = ry[e, r:r + 1, :] + ry[E8 + e, r:r + 1, :]
+        rzs[r] = jnp.concatenate([tile[r:r + 1] for tile in by_sender], axis=0)
     for i in range(ZS - 1):
         rz_copy(i).start()
     rz[z] = rzs[0]
@@ -534,9 +532,9 @@
     value = jnp.zeros((EXP, TOK), F32)
     for p in range(CAP):
         value = jnp.where(qt2 == float(p), by_expert[:, p:p + 1], value)
-    for k in range(TOP):
-        gg[x, k:k + 1, :] = jnp.sum(
-            jnp.where(routes_ref[k:k + 1, :] == eidx, value, 0.0), axis=0, keepdims=True)
+    found = [
+        jnp.sum(jnp.where(routes_v[k:k + 1, :] == eidx, value, 0.0), axis=0, keepdims=True) for k in range(TOP)]
+    gg[x, 0:TOP, :] = jnp.concatenate(found, axis=0)
     gg[x, 8:16, :] = jnp.broadcast_to(
         jnp.sum(by_expert[:, TOK - 1:TOK], axis=0, keepdims=True), (8, TOK))
     for i in range(XS - 1):
@@ -598,6 +596,7 @@
     most = max(TPS, HS * E8, ZS)
     any_space = pl.BlockSpec(memory_space=pl.ANY)
     in_hbm = pl.BlockSpec(memory_space=pltpu.HBM)
+    held = lambda a: pltpu.with_memory_space_constraint(a, pltpu.HBM)
     in_vmem = pl.BlockSpec(memory_space=pltpu.VMEM)
     part, factor, gate_grad = pl.pallas_call(
         kernel,
@@ -606,11 +605,10 @@
             jax.ShapeDtypeStruct((8, 128), F32),
             jax.ShapeDtypeStruct((TOP, TOK), F32),
         ),
-        in_specs=[in_hbm] * 5,
+        in_specs=[in_hbm, in_vmem, in_hbm, in_hbm, in_hbm],
         out_specs=(any_space, in_vmem, in_vmem),
         scratch_shapes=[
             vm((TOP, TOK), jnp.int32),
-            vm((TOP, TOK), BF16),
             vm((NR, ZS * TOK, DR), BF16),
             [vm((E8 * n, k * TOK), BF16) for n, k in zip(sizes, reach)],
             vm((NQ, E8, ZS * CAP, DQ), BF16),
@@ -623,7 +621,7 @@
             vm((SLOTS, SLOTS), BF16),
             vm((XS * FFD, SLOTS), BF16),
             vm((XS * FFD, SLOTS), BF16),
-            vm((XS, SLOTS, FFD), BF16),
+            vm((XS, SLOTS, -(-FFD // 128) * 128), BF16),
             vm((NQ, XS * FFD, DQ), BF16),
             vm((NQ, XS * FFD, DQ), BF16),
             vm((NQ, SLOTS, DQ), F32),
@@ -634,7 +632,7 @@
             vm((ZS, E8, TOK), F32),
             vm((ZS, E8, TOK), F32),
             vm((XS, 16, TOK), F32),
-            dma((3 + NR + 2 * NQ + NQ * GROUPS,)),
+            dma((2 + NR + 2 * NQ + NQ * GROUPS,)),
             dma((NR, ZS)),
             dma((NR, ZS)),
             dma((NQ, GROUPS, E8)),
@@ -655,7 +653,8 @@
         cost_estimate=pl.CostEstimate(
             flops=2 * 2 * SLOTS * FFD * D, bytes_accessed=8 * 1024 * 1024, transcendentals=0),
         name="moe_down_backward",
-    )(*[pltpu.with_memory_space_constraint(a, pltpu.HBM) for a in (routes.T, gates.T, grad_out, hidden, w_down)])
+    )(
+        held(routes.T), gates.T, held(grad_out), held(hidden), held(w_down))
     high = 32 if FFD % 32 == 0 else FFD
     down_grad, gate_grad = pl.pallas_call(
         scale_kernel,

time: 72.7 us -> 73.3 us (level)
  no operation moved by 1% of the time
where the time goes in v6:
time: 73.3 us; the launch traced here: 73.2 us
  Pallas kernels  71.9 us (98%)
    pallas_call x1, Pallas kernels, per_device(): pl.pallas_call(kernel, out_shape=(jax.ShapeDtypeStruct((1, FFD, D), BF16)...  70.6 us

profile of v6, /device:TPU:1, one launch (start us, length us, event | category | flops | bytes accessed | tf_op | source)
XLA Modules:
  0.0 73.2 jit_solution(6753621535126709074)
XLA Ops:
  0.6 0.0 copy-start
  0.6 0.7 copy-done
  1.3 70.6 %moe_down_backward.1 = (bf16[1,192,4096]{2,1,0:T(8,128)(2,1)S(1)}, f32[8,128]{1,0:T(8,128)S(1)}, f32[8,128]{1,0:T(8,128)S(1)}) custom-call(s32[8,128]{1,0:T(8,128)} %bitcast.4, bf16[8,128]{1,0:T(8,128)(2,1)S(1)} %bitcast.3, bf16[128,4096]{1,0:T(8,128)(2,1)} %grad_hbm.1, bf16[1,192,1280]{2,1,0:T(8,128)(2,1)} %hid_hbm.1, bf16[1,192,4096]{2,1,0:T(8,128)(2,1)} %w_hbm.1), custom_call_target="tpu_custom_call" | custom-call | flops 4026531840 | bytes 8388608 | tf_op jit(solution)/shard_map/moe_down_backward/pallas_call | solution.py:601
  71.9 1.3 %scale_products.1 = (bf16[1,192,4096]{2,1,0:T(8,128)(2,1)}, f32[8,128]{1,0:T(8,128)}) custom-call(bf16[1,192,4096]{2,1,0:T(8,128)(2,1)S(1)} %get-tuple-element.7.part_ref, f32[8,128]{1,0:T(8,128)S(1)} %get-tuple-element.8.factor_ref, f32[8,128]{1,0:T(8,128)S(1)} %get-tuple-element.9.gg_in), custom_call_target="tpu_custom_call" | custom-call | flops 786432 | bytes 3145728 | tf_op jit(solution)/shard_map/scale_products/pallas_call | solution.py:659
Async XLA Ops:
  0.6 0.7 copy-start

commit v7 on v6

--- a/solution.py
+++ b/solution.py
@@ -443,7 +443,8 @@
 
     def products(q, squares):
         wait_rows(q)
-        for i in near_x + [XS - 1] + [i for i in range(XS - 1) if i not in near_x]:
+        far_x = [i for i in range(XS - 1) if i not in near_x]
+        for i in near_x + [XS - 1] + far_x if q == 0 else far_x + near_x + [XS - 1]:
             there = x if i == XS - 1 else peers_x[i][1]
             if i not in near_x and i < XS - 1 and q == 0:
                 get_far()

time: 73.3 us -> 73.2 us (level)
  no operation moved by 1% of the time
where the time goes in v7:
time: 73.2 us; the launch traced here: 73.1 us
  Pallas kernels  71.8 us (98%)
    pallas_call x1, Pallas kernels, per_device(): pl.pallas_call(kernel, out_shape=(jax.ShapeDtypeStruct((1, FFD, D), BF16)...  70.5 us

profile of v7, /device:TPU:1, one launch (start us, length us, event | category | flops | bytes accessed | tf_op | source)
XLA Modules:
  0.0 73.1 jit_solution(9512405219825507681)
XLA Ops:
  0.6 0.0 copy-start
  0.6 0.7 copy-done
  1.3 70.5 %moe_down_backward.1 = (bf16[1,192,4096]{2,1,0:T(8,128)(2,1)S(1)}, f32[8,128]{1,0:T(8,128)S(1)}, f32[8,128]{1,0:T(8,128)S(1)}) custom-call(s32[8,128]{1,0:T(8,128)} %bitcast.4, bf16[8,128]{1,0:T(8,128)(2,1)S(1)} %bitcast.3, bf16[128,4096]{1,0:T(8,128)(2,1)} %grad_hbm.1, bf16[1,192,1280]{2,1,0:T(8,128)(2,1)} %hid_hbm.1, bf16[1,192,4096]{2,1,0:T(8,128)(2,1)} %w_hbm.1), custom_call_target="tpu_custom_call" | custom-call | flops 4026531840 | bytes 8388608 | tf_op jit(solution)/shard_map/moe_down_backward/pallas_call | solution.py:602
  71.8 1.3 %scale_products.1 = (bf16[1,192,4096]{2,1,0:T(8,128)(2,1)}, f32[8,128]{1,0:T(8,128)}) custom-call(bf16[1,192,4096]{2,1,0:T(8,128)(2,1)S(1)} %get-tuple-element.7.part_ref, f32[8,128]{1,0:T(8,128)S(1)} %get-tuple-element.8.factor_ref, f32[8,128]{1,0:T(8,128)S(1)} %get-tuple-element.9.gg_in), custom_call_target="tpu_custom_call" | custom-call | flops 786432 | bytes 3145728 | tf_op jit(solution)/shard_map/scale_products/pallas_call | solution.py:660
Async XLA Ops:
  0.6 0.7 copy-start
